TPU v7x, 128 devices: a whole 4x4x4 slice. The times are simulated.
128 devices in a mesh: dp: 16 (over x, y_lo, core), tensor: 8 (over y_hi, z).
Axes of the slice: x: 4, y: 4 (y_hi: 2, y_lo: 2; y = y_hi * 2 + y_lo), z: 4, core: 2. Of those that a mesh axis runs over, the one named last changes fastest.
Arguments:
- layer_input: bfloat16 [16384, 1024], P(('dp', 'tensor')), may hold values from -6 to 6
- seq_lengths: int32 [16, 4], P('dp'), may hold values from 1 to 1021, as said below
- attn_gain: bfloat16 [1024], P('dp'), may hold values from 0.099609375 to 1.8984375
- w_query: bfloat16 [1024, 2048], P('dp', 'tensor'), may hold values from -0.1875 to 0.1875
- key_projection: bfloat16 [1024, 1024], P('dp', 'tensor'), may hold values from -0.1875 to 0.1875
- value_projection: bfloat16 [1024, 1024], P('dp', 'tensor'), may hold values from -0.1875 to 0.1875
- query_gain: bfloat16 [128], replicated, may hold values from 0.25 to 1.75
- key_gain: bfloat16 [128], replicated, may hold values from 0.25 to 1.75
- w_out: bfloat16 [2048, 1024], P('tensor', 'dp'), may hold values from -1 to 1
- mlp_gain: bfloat16 [1024], P('dp'), may hold values from 0.099609375 to 1.8984375
- w_gate: bfloat16 [1024, 3072], P('dp', 'tensor'), may hold values from -0.1875 to 0.1875
- w_up: bfloat16 [1024, 3072], P('dp', 'tensor'), may hold values from -0.1875 to 0.1875
- w_down: bfloat16 [3072, 1024], P('tensor', 'dp'), may hold values from -0.109375 to 0.109375
- out_grad: bfloat16 [16384, 1024], P(('dp', 'tensor')), may hold values from -6 to 6
Outputs:
- layer_output: bfloat16 [16384, 1024], P(('dp', 'tensor'))
- input_grad: bfloat16 [16384, 1024], P(('dp', 'tensor'))
- grad_attn_gain: float32 [1024], P('dp')
- grad_query_w: float32 [1024, 2048], P('dp', 'tensor')
- grad_key_w: float32 [1024, 1024], P('dp', 'tensor')
- grad_value_w: float32 [1024, 1024], P('dp', 'tensor')
- grad_query_gain: float32 [128], replicated
- grad_key_gain: float32 [128], replicated
- grad_out_w: float32 [2048, 1024], P('tensor', 'dp')
- grad_mlp_gain: float32 [1024], P('dp')
- grad_gate_w: float32 [1024, 3072], P('dp', 'tensor')
- grad_up_w: float32 [1024, 3072], P('dp', 'tensor')
- grad_down_w: float32 [3072, 1024], P('tensor', 'dp')
Inputs may be any that keep to these rules, and one draw needn't show every extreme that they name: `seq_lengths`: row r lists the lengths of the 4 documents packed in order into the 1024 tokens of dp index r and sums to 1024. In every row one document, which one drawn, begins among the first 128 of those tokens and ends among the last 128; every other one has at most (127) // 3 tokens.
All inputs are finite; a program needn't handle non-finite values.
Results may differ from a plain program's by a relative error of at most 0.025.
Values may be sent and summed in bfloat16 or wider, within the bound.
A program may use at most 128 MiB of HBM per device.

v0:
```python
import jax
import jax.numpy as jnp
from jax import lax
from jax.sharding import PartitionSpec as P

QUERY_HEADS = 16
KEY_VALUE_HEADS = 8
HEAD_SIZE = 128


eps_norm = 1e-06
rope_base = 1000000.0
masked_score = -1e30


def rms_scale(values, gain_in):
    return (
        values * lax.rsqrt(jnp.mean(values * values, axis=-1, keepdims=True) + eps_norm) * gain_in
    )


def rotate(values, cosine, sine_table):
    half_width = values.shape[-1] // 2
    turned = jnp.concatenate([-values[..., half_width:], values[..., :half_width]], axis=-1)
    return values * cosine + turned * sine_table


def tables(positions, head_width):
    frequency = rope_base ** (-(jnp.arange(head_width // 2).astype(jnp.float32) * 2.0 / head_width))
    angles = positions.astype(jnp.float32)[:, None] * frequency[None, :]
    cosine = jnp.concatenate([jnp.cos(angles), jnp.cos(angles)], axis=-1)
    sine_table = jnp.concatenate([jnp.sin(angles), jnp.sin(angles)], axis=-1)
    return (cosine[:, None, :], sine_table[:, None, :])


def layout(lengths, row_count):
    doc_ends = jnp.cumsum(lengths)
    doc_starts = doc_ends - lengths
    row_position = jnp.arange(row_count, dtype=jnp.int32)
    document_labels = jnp.sum(
        (row_position[:, None] >= doc_ends[None, :]).astype(jnp.int32), axis=1
    )
    chosen = document_labels[:, None] == jnp.arange(lengths.shape[0], dtype=jnp.int32)[None, :]
    offsets = jnp.sum(jnp.where(chosen, doc_starts[None, :], 0), axis=1)
    return (document_labels, row_position - offsets, row_position)


def rows_times(left, right):
    return lax.dot_general(
        left, right, (((1,), (1,)), ((), ())), preferred_element_type=jnp.float32
    )


def cols_times(left, right):
    return lax.dot_general(
        left, right, (((0,), (0,)), ((), ())), preferred_element_type=jnp.float32
    )


def per_device(
    layer_input,
    seq_lengths,
    attn_gain,
    w_query,
    key_projection,
    value_projection,
    query_gain,
    key_gain,
    w_out,
    mlp_gain,
    w_gate,
    w_up,
    w_down,
    out_grad,
):
    tensor_shard_count = lax.axis_size("tensor")
    rows_own = layer_input.shape[0]
    group_rows = rows_own * tensor_shard_count
    heads_local = QUERY_HEADS // tensor_shard_count
    local_key_value = KEY_VALUE_HEADS // tensor_shard_count
    repeat_factor = QUERY_HEADS // KEY_VALUE_HEADS
    scaling = HEAD_SIZE ** (-0.5)
    block_rows = group_rows // max(1, group_rows // 512)
    block_count = group_rows // block_rows
    (
        query_full,
        key_full,
        value_full,
        gate_full,
        up_full,
        out_full,
        down_full,
        gain_attn,
        gain_mlp,
    ) = (
        lax.all_gather(w_query, "dp", axis=0, tiled=True),
        lax.all_gather(key_projection, "dp", axis=0, tiled=True),
        lax.all_gather(value_projection, "dp", axis=0, tiled=True),
        lax.all_gather(w_gate, "dp", axis=0, tiled=True),
        lax.all_gather(w_up, "dp", axis=0, tiled=True),
        lax.all_gather(w_out.T, "dp", axis=0, tiled=True),
        lax.all_gather(w_down.T, "dp", axis=0, tiled=True),
        lax.all_gather(attn_gain, "dp", axis=0, tiled=True),
        lax.all_gather(mlp_gain, "dp", axis=0, tiled=True),
    )
    gain_attn = gain_attn.astype(jnp.float32)
    gain_mlp = gain_mlp.astype(jnp.float32)
    gain_query = query_gain.astype(jnp.float32)
    gain_key = key_gain.astype(jnp.float32)
    document_labels, positions, row_position = layout(seq_lengths[0], group_rows)
    cosine, sine_table = tables(positions, HEAD_SIZE)
    own_input = layer_input.astype(jnp.float32)
    first_normalized = rms_scale(own_input, gain_attn).astype(jnp.bfloat16)
    hidden_one = lax.all_gather(first_normalized, "tensor", axis=0, tiled=True)
    query_pre = jnp.dot(hidden_one, query_full, preferred_element_type=jnp.float32)
    key_before_rotary = jnp.dot(hidden_one, key_full, preferred_element_type=jnp.float32)
    value_row_matrix = (
        jnp.dot(hidden_one, value_full, preferred_element_type=jnp.float32)
        .astype(jnp.bfloat16)
        .reshape(group_rows, local_key_value, HEAD_SIZE)
    )

    def query_piece(pre_in, gain_in):
        return rotate(
            rms_scale(pre_in.reshape(group_rows, heads_local, HEAD_SIZE), gain_in),
            cosine,
            sine_table,
        )

    def key_piece(pre_in, gain_in):
        return rotate(
            rms_scale(pre_in.reshape(group_rows, local_key_value, HEAD_SIZE), gain_in),
            cosine,
            sine_table,
        )

    query_rotated = (
        query_piece(query_pre, gain_query)
        .astype(jnp.bfloat16)
        .reshape(group_rows, local_key_value, repeat_factor, HEAD_SIZE)
    )
    key_rotated = key_piece(key_before_rotary, gain_key).astype(jnp.bfloat16)

    def scores_for(query_tile_rows, doc_block, index_block):
        raw_scores = (
            jnp.einsum(
                "qgrd,kgd->grqk", query_tile_rows, key_rotated, preferred_element_type=jnp.float32
            )
            * scaling
        )
        allowed = (doc_block[:, None] == document_labels[None, :]) & (
            row_position[None, :] <= index_block[:, None]
        )
        return jnp.where(allowed[None, None], raw_scores, masked_score)

    def forward_block(block_item):
        query_tile_rows, doc_block, index_block = block_item
        scores = scores_for(query_tile_rows, doc_block, index_block)
        row_max = jnp.max(scores, axis=-1, keepdims=True)
        exp_terms = jnp.exp(scores - row_max)
        row_total = jnp.sum(exp_terms, axis=-1, keepdims=True)
        weights = (exp_terms / row_total).astype(jnp.bfloat16)
        mixed_block = jnp.einsum(
            "grqk,kgd->qgrd", weights, value_row_matrix, preferred_element_type=jnp.float32
        )
        return (mixed_block.astype(jnp.bfloat16), row_max + jnp.log(row_total))

    query_blocks = query_rotated.reshape(
        block_count, block_rows, local_key_value, repeat_factor, HEAD_SIZE
    )
    doc_blocks = document_labels.reshape(block_count, block_rows)
    index_blocks = row_position.reshape(block_count, block_rows)
    mixed_out, log_total = lax.map(forward_block, (query_blocks, doc_blocks, index_blocks))
    mixed_out = mixed_out.reshape(group_rows, heads_local * HEAD_SIZE)
    middle = own_input + lax.psum_scatter(
        rows_times(mixed_out, out_full).astype(jnp.bfloat16),
        "tensor",
        scatter_dimension=0,
        tiled=True,
    ).astype(jnp.float32)
    normed_two = rms_scale(middle, gain_mlp).astype(jnp.bfloat16)
    hidden_two = lax.all_gather(normed_two, "tensor", axis=0, tiled=True)
    gate_pre = jnp.dot(hidden_two, gate_full, preferred_element_type=jnp.float32)
    up_pre = jnp.dot(hidden_two, up_full, preferred_element_type=jnp.float32)
    activated = (jax.nn.silu(gate_pre) * up_pre).astype(jnp.bfloat16)
    output = middle + lax.psum_scatter(
        rows_times(activated, down_full).astype(jnp.bfloat16),
        "tensor",
        scatter_dimension=0,
        tiled=True,
    ).astype(jnp.float32)
    layer_output = output.astype(jnp.bfloat16)
    grad_rows = lax.all_gather(out_grad, "tensor", axis=0, tiled=True)
    grad_act = jnp.dot(grad_rows, down_full, preferred_element_type=jnp.float32)
    unused, swiglu_back = jax.vjp(
        lambda gate_in, up_in: jax.nn.silu(gate_in) * up_in, gate_pre, up_pre
    )
    grad_gate, grad_up = swiglu_back(grad_act)
    grad_gate = grad_gate.astype(jnp.bfloat16)
    grad_up = grad_up.astype(jnp.bfloat16)
    grad_gate_full = cols_times(hidden_two, grad_gate)
    grad_up_full = cols_times(hidden_two, grad_up)
    grad_down_full = cols_times(grad_rows, activated)
    grad_norm_two = lax.psum_scatter(
        (rows_times(grad_gate, gate_full) + rows_times(grad_up, up_full)).astype(jnp.bfloat16),
        "tensor",
        scatter_dimension=0,
        tiled=True,
    ).astype(jnp.float32)
    unused, norm_two_back = jax.vjp(rms_scale, middle, gain_mlp)
    grad_middle_norm, grad_gain_two = norm_two_back(grad_norm_two)
    grad_middle = out_grad.astype(jnp.float32) + grad_middle_norm
    grad_branch = lax.all_gather(grad_middle.astype(jnp.bfloat16), "tensor", axis=0, tiled=True)
    grad_out_full = cols_times(grad_branch, mixed_out)
    grad_mixed = jnp.dot(grad_branch, out_full, preferred_element_type=jnp.float32).astype(
        jnp.bfloat16
    )
    grad_mixed_blocks = grad_mixed.reshape(
        block_count, block_rows, local_key_value, repeat_factor, HEAD_SIZE
    )

    def backward_block(carried, block_item):
        grad_keys, grad_values = carried
        query_tile_rows, doc_block, index_block, grad_block, log_block = block_item
        scores = scores_for(query_tile_rows, doc_block, index_block)
        probs_full = jnp.exp(scores - log_block)
        grad_probs = jnp.einsum(
            "qgrd,kgd->grqk", grad_block, value_row_matrix, preferred_element_type=jnp.float32
        )
        inner_sum = jnp.sum(probs_full * grad_probs, axis=-1, keepdims=True)
        grad_scores = (probs_full * (grad_probs - inner_sum)).astype(jnp.bfloat16)
        grad_query = (
            jnp.einsum(
                "grqk,kgd->qgrd", grad_scores, key_rotated, preferred_element_type=jnp.float32
            )
            * scaling
        )
        grad_keys = (
            grad_keys
            + jnp.einsum(
                "grqk,qgrd->kgd", grad_scores, query_tile_rows, preferred_element_type=jnp.float32
            )
            * scaling
        )
        grad_values = grad_values + jnp.einsum(
            "grqk,qgrd->kgd",
            probs_full.astype(jnp.bfloat16),
            grad_block,
            preferred_element_type=jnp.float32,
        )
        return ((grad_keys, grad_values), grad_query)

    zero_state = jnp.zeros((group_rows, local_key_value, HEAD_SIZE), jnp.float32)
    (grad_keys, grad_values), grad_queries = lax.scan(
        backward_block,
        (zero_state, zero_state),
        (query_blocks, doc_blocks, index_blocks, grad_mixed_blocks, log_total),
    )
    grad_query_rot = lax.optimization_barrier(
        grad_queries.reshape(group_rows, heads_local, HEAD_SIZE).astype(jnp.bfloat16)
    ).astype(jnp.float32)
    grad_key_rot = lax.optimization_barrier(grad_keys.astype(jnp.bfloat16)).astype(jnp.float32)
    grad_values = grad_values.astype(jnp.bfloat16).reshape(group_rows, local_key_value * HEAD_SIZE)
    unused, query_back = jax.vjp(query_piece, query_pre, gain_query)
    grad_query_pre, grad_gain_query = query_back(grad_query_rot)
    unused, key_back = jax.vjp(key_piece, key_before_rotary, gain_key)
    grad_key_pre, grad_gain_key = key_back(grad_key_rot)
    grad_query_pre = grad_query_pre.astype(jnp.bfloat16)
    grad_key_pre = grad_key_pre.astype(jnp.bfloat16)
    grad_query_full = cols_times(hidden_one, grad_query_pre)
    grad_key_full = cols_times(hidden_one, grad_key_pre)
    grad_value_full = cols_times(hidden_one, grad_values)
    grad_norm_one = lax.psum_scatter(
        (
            rows_times(grad_query_pre, query_full)
            + rows_times(grad_key_pre, key_full)
            + rows_times(grad_values, value_full)
        ).astype(jnp.bfloat16),
        "tensor",
        scatter_dimension=0,
        tiled=True,
    ).astype(jnp.float32)
    unused, norm_one_back = jax.vjp(rms_scale, own_input, gain_attn)
    grad_input_norm, grad_gain_one = norm_one_back(grad_norm_one)
    input_grad = (grad_middle + grad_input_norm).astype(jnp.bfloat16)
    total_one, total_two, total_query, total_key = lax.psum(
        (grad_gain_one, grad_gain_two, grad_gain_query, grad_gain_key), ("dp", "tensor")
    )
    gain_piece = attn_gain.shape[0]
    gain_start = lax.axis_index("dp") * gain_piece
    shard_gain_one = lax.dynamic_slice_in_dim(total_one, gain_start, gain_piece, 0)
    shard_gain_two = lax.dynamic_slice_in_dim(total_two, gain_start, gain_piece, 0)
    shard_query, shard_key, shard_value, shard_gate, shard_up, shard_out, shard_down = (
        lax.psum_scatter(
            grad_query_full.astype(jnp.bfloat16), "dp", scatter_dimension=0, tiled=True
        ).astype(jnp.float32),
        lax.psum_scatter(
            grad_key_full.astype(jnp.bfloat16), "dp", scatter_dimension=0, tiled=True
        ).astype(jnp.float32),
        lax.psum_scatter(
            grad_value_full.astype(jnp.bfloat16), "dp", scatter_dimension=0, tiled=True
        ).astype(jnp.float32),
        lax.psum_scatter(
            grad_gate_full.astype(jnp.bfloat16), "dp", scatter_dimension=0, tiled=True
        ).astype(jnp.float32),
        lax.psum_scatter(
            grad_up_full.astype(jnp.bfloat16), "dp", scatter_dimension=0, tiled=True
        ).astype(jnp.float32),
        lax.psum_scatter(
            grad_out_full.astype(jnp.bfloat16), "dp", scatter_dimension=0, tiled=True
        ).astype(jnp.float32),
        lax.psum_scatter(
            grad_down_full.astype(jnp.bfloat16), "dp", scatter_dimension=0, tiled=True
        ).astype(jnp.float32),
    )
    return (
        layer_output,
        input_grad,
        shard_gain_one,
        shard_query,
        shard_key,
        shard_value,
        total_query,
        total_key,
        shard_out.T,
        shard_gain_two,
        shard_gate,
        shard_up,
        shard_down.T,
    )


def solution(mesh):
    in_specs = (
        P(("dp", "tensor"), None),
        P("dp", None),
        P("dp"),
        P("dp", "tensor"),
        P("dp", "tensor"),
        P("dp", "tensor"),
        P(),
        P(),
        P("tensor", "dp"),
        P("dp"),
        P("dp", "tensor"),
        P("dp", "tensor"),
        P("tensor", "dp"),
        P(("dp", "tensor"), None),
    )
    out_specs = (
        P(("dp", "tensor"), None),
        P(("dp", "tensor"), None),
        P("dp"),
        P("dp", "tensor"),
        P("dp", "tensor"),
        P("dp", "tensor"),
        P(),
        P(),
        P("tensor", "dp"),
        P("dp"),
        P("dp", "tensor"),
        P("dp", "tensor"),
        P("tensor", "dp"),
    )
    return jax.shard_map(
        per_device, mesh=mesh, in_specs=in_specs, out_specs=out_specs, check_vma=False
    )
```

profile of v0, /device:TPU:1, one launch (start us, length us, event | category | flops | bytes accessed | tf_op | source)
XLA Modules:
  0.0 1098.0 jit_solution(10029622868177456160)
XLA Ops:
  12.0 28.6 %all-reduce.7 = (bf16[1024]{0:T(1024)(128)(2,1)S(1)}, bf16[1024]{0:T(1024)(128)(2,1)}) all-reduce(bf16[1024]{0:T(1024)(128)(2,1)S(1)} %dynamic-update-slice, bf16[1024]{0:T(1024)(128)(2,1)S(1)} %dynamic-update-slice.1), channel_id=1, replica_groups=mesh['dp'=16,'tensor'=8] {'dp'}, use_global_device_ids=true, to_apply=%add.4 | all-reduce | flops 2048 | bytes 8192
  46.1 20.7 %all_gather.42 = bf16[1024,128]{1,0:T(8,128)(2,1)S(1)} all-gather(bf16[64,128]{1,0:T(8,128)(2,1)} %param.22), channel_id=1, replica_groups=mesh['dp'=16,'tensor'=8] {'dp'}, dimensions={0}, use_global_device_ids=true | all-gather | bytes 278528 | tf_op jit(solution)/shard_map/all_gather | solution.py:97
  66.8 20.6 %all_gather.43 = bf16[1024,128]{1,0:T(8,128)(2,1)} all-gather(bf16[64,128]{1,0:T(8,128)(2,1)} %param.23), channel_id=1, replica_groups=mesh['dp'=16,'tensor'=8] {'dp'}, dimensions={0}, use_global_device_ids=true | all-gather | bytes 278528 | tf_op jit(solution)/shard_map/all_gather | solution.py:98
  87.4 4.0 multiply_cosine_fusion.1
  93.7 19.1 %all_gather.41 = bf16[1024,256]{1,0:T(8,128)(2,1)} all-gather(bf16[64,256]{1,0:T(8,128)(2,1)S(1)} %copy-done.45), channel_id=1, replica_groups=mesh['dp'=16,'tensor'=8] {'dp'}, dimensions={0}, use_global_device_ids=true | all-gather | bytes 557056 | tf_op jit(solution)/shard_map/all_gather | solution.py:96
  112.8 21.1 %all_gather.44 = bf16[1024,256]{1,0:T(8,128)(2,1)} all-gather(bf16[64,256]{1,0:T(8,128)(2,1)S(1)} %bitcast.361), channel_id=1, replica_groups=mesh['dp'=16,'tensor'=8] {'dp'}, dimensions={0}, use_global_device_ids=true | all-gather | bytes 557056 | tf_op jit(solution)/shard_map/all_gather | solution.py:101
  148.1 4.2 fusion.69
  156.7 13.1 %while.28 = (s32[]{:T(128)}, bf16[2,512,1,2,128]{4,3,1,0,2:T(2,128)(2,1)}, f32[2,1,2,512,1]{3,2,4,1,0:T(2,128)S(1)}, s32[2,512]{1,0:T(2,128)S(1)}, s32[1024]{0:T...) while((s32[]{:T(128)}, ...), condition=%wide.region_9.10_spmd.clone, body=%wide.region_6.9_spmd.clone.sunk | while | flops 551156736 | bytes 21545168 | solution.py:173
  169.8 3.3 convolution_convert_fusion.1
  173.9 72.4 %reduce-scatter.14.cloned.1.call-done = bf16[128,1024]{1,0:T(8,128)(2,1)} async-done(((bf16[1024,1024]{1,0:T(8,128)(2,1)}), bf16[128,1024]{1,0:T(8,128)(2,1)}) %reduce-scatter.14.cloned.1.call-update) | async-done | bytes 262160 | tf_op jit(solution)/shard_map/reduce_scatter | solution.py:175
  251.0 24.3 %all_gather.47 = bf16[1024,384]{1,0:T(8,128)(2,1)} all-gather(bf16[64,384]{1,0:T(8,128)(2,1)S(1)} %copy-done.43), channel_id=1, replica_groups=mesh['dp'=16,'tensor'=8] {'dp'}, dimensions={0}, use_global_device_ids=true | all-gather | bytes 835584 | tf_op jit(solution)/shard_map/all_gather | solution.py:99
  275.3 20.4 %all_gather.48 = bf16[1024,384]{1,0:T(8,128)(2,1)} all-gather(bf16[64,384]{1,0:T(8,128)(2,1)S(1)} %copy-done.44), channel_id=1, replica_groups=mesh['dp'=16,'tensor'=8] {'dp'}, dimensions={0}, use_global_device_ids=true | all-gather | bytes 835584 | tf_op jit(solution)/shard_map/all_gather | solution.py:100
  295.7 23.3 %all_gather.49 = bf16[1024,384]{1,0:T(8,128)(2,1)} all-gather(bf16[64,384]{1,0:T(8,128)(2,1)} %bitcast.360), channel_id=1, replica_groups=mesh['dp'=16,'tensor'=8] {'dp'}, dimensions={0}, use_global_device_ids=true | all-gather | bytes 835584 | tf_op jit(solution)/shard_map/all_gather | solution.py:102
  319.0 4.4 fusion.110
  325.9 38.1 %all-gather.9.cloned.1.call-done = bf16[1024,1024]{1,0:T(8,128)(2,1)} async-done(((bf16[128,1024]{1,0:T(8,128)(2,1)}), bf16[1024,1024]{1,0:T(8,128)(2,1)}) %all-gather.9.cloned.1.call-update) | async-done | bytes 2097168 | tf_op jit(solution)/shard_map/all_gather | solution.py:193
  364.0 5.5 multiply_convert_fusion
  373.9 72.0 %reduce-scatter.18.cloned.1.call-done = bf16[128,1024]{1,0:T(8,128)(2,1)} async-done(((bf16[1024,1024]{1,0:T(8,128)(2,1)}), bf16[128,1024]{1,0:T(8,128)(2,1)}) %reduce-scatter.18.cloned.1.call-update) | async-done | bytes 262160 | tf_op jit(solution)/shard_map/reduce_scatter | solution.py:204
  449.5 3.7 fusion.63
  455.6 4.0 convolution_convert_fusion.3
  459.6 4.0 convolution_convert_fusion.4
  464.0 39.5 %all-gather.11.cloned.1.call-done = bf16[1024,1024]{1,0:T(8,128)(2,1)} async-done(((bf16[128,1024]{1,0:T(8,128)(2,1)}), bf16[1024,1024]{1,0:T(8,128)(2,1)}) %all-gather.11.cloned.1.call-update) | async-done | bytes 2097168 | tf_op jit(solution)/shard_map/all_gather | solution.py:213
  508.6 21.7 %while.29 = (s32[]{:T(128)}, f32[1024,1,128]{0,2,1:T(8,128)}, f32[1024,1,128]{0,2,1:T(8,128)}, bf16[2,512,1,2,128]{4,1,0,3,2:T(8,128)(2,1)}, bf16[2,512,1,2,128]...) while((s32[]{:T(128)}, f32[1024,1,128]{0,2,1:T(8,128)}, ...), condition=%wide.region_17.18_spmd.clone, body=%wide.region_15.17_spmd.clone.sunk | while | flops 1360264192 | bytes 54309260 | solution.py:254
  550.1 3.2 convolution_convert_fusion.5
  563.6 60.0 %reduce-scatter.32.cloned.1.call-done = bf16[64,384]{1,0:T(8,128)(2,1)} async-done(((bf16[1024,384]{1,0:T(8,128)(2,1)}), bf16[64,384]{1,0:T(8,128)(2,1)}) %reduce-scatter.32.cloned.1.call-update) | async-done | bytes 49168 | tf_op jit(solution)/shard_map/reduce_scatter | solution.py:306
  625.0 60.6 %reduce-scatter.30.cloned.1.call-done = bf16[64,384]{1,0:T(8,128)(2,1)} async-done(((bf16[1024,384]{1,0:T(8,128)(2,1)}), bf16[64,384]{1,0:T(8,128)(2,1)}) %reduce-scatter.30.cloned.1.call-update) | async-done | bytes 49168 | tf_op jit(solution)/shard_map/reduce_scatter | solution.py:303
  687.1 60.1 %reduce-scatter.24.cloned.1.call-done = bf16[64,128]{1,0:T(8,128)(2,1)} async-done(((bf16[1024,128]{1,0:T(8,128)(2,1)}), bf16[64,128]{1,0:T(8,128)(2,1)}) %reduce-scatter.24.cloned.1.call-update) | async-done | bytes 16400 | tf_op jit(solution)/shard_map/reduce_scatter | solution.py:297
  748.5 59.5 %reduce-scatter.26.cloned.1.call-done = bf16[64,128]{1,0:T(8,128)(2,1)} async-done(((bf16[1024,128]{1,0:T(8,128)(2,1)}), bf16[64,128]{1,0:T(8,128)(2,1)}) %reduce-scatter.26.cloned.1.call-update) | async-done | bytes 16400 | tf_op jit(solution)/shard_map/reduce_scatter | solution.py:300
  809.4 60.0 %reduce-scatter.22.cloned.1.call-done = bf16[64,256]{1,0:T(8,128)(2,1)} async-done(((bf16[1024,256]{1,0:T(8,128)(2,1)}), bf16[64,256]{1,0:T(8,128)(2,1)}) %reduce-scatter.22.cloned.1.call-update) | async-done | bytes 32784 | tf_op jit(solution)/shard_map/reduce_scatter | solution.py:294
  870.8 60.1 %reduce-scatter.28.cloned.1.call-done = bf16[64,256]{1,0:T(8,128)(2,1)} async-done(((bf16[1024,256]{1,0:T(8,128)(2,1)}), bf16[64,256]{1,0:T(8,128)(2,1)}) %reduce-scatter.28.cloned.1.call-update) | async-done | bytes 32784 | tf_op jit(solution)/shard_map/reduce_scatter | solution.py:309
  932.3 78.6 %reduce-scatter.20.cloned.1.call-done = bf16[128,1024]{1,0:T(8,128)(2,1)} async-done(((bf16[1024,1024]{1,0:T(8,128)(2,1)}), bf16[128,1024]{1,0:T(8,128)(2,1)}) %reduce-scatter.20.cloned.1.call-update) | async-done | bytes 262160 | tf_op jit(solution)/shard_map/reduce_scatter | solution.py:273
  1012.1 67.5 %all-reduce.6 = (f32[1024]{0:T(1024)S(1)}, f32[128]{0:T(128)}, f32[128]{0:T(128)}, f32[1024]{0:T(1024)S(1)}) all-reduce(f32[1024]{0:T(1024)S(1)} %get-tuple-element.411, f32[128]{0:T(128)S(1)} %get-tuple-element.405, f32[128]{0:T(128)S(1)} %get-tuple-element.407, ...), channel_id=1, replica_groups=mesh['dp'=16,'tensor'=8] {'dp','tensor'}, use_global_device_ids=true, to_apply=%region_23.24 | all-reduce | flops 2304 | bytes 18432 | tf_op jit(solution)/shard_map/psum | solution.py:286
  1080.7 8.3 reduce-scatter.16.cloned.1.call-done
  (299 shorter events, 131.0 us)
Async XLA Ops:
  7.2 126.8 %all-gather.5.cloned.1.call-start = ((), (), s32[]{:S(2)}) async-start(), calls=%async_computation.11 | async-start | bytes 2359296 | tf_op jit(solution)/shard_map/all_gather | solution.py:114
  8.3 85.4 %copy-start.45 = (bf16[64,256]{1,0:T(8,128)(2,1)S(1)}, bf16[64,256]{1,0:T(8,128)(2,1)}, u32[]{:S(2)}) copy-start(bf16[64,256]{1,0:T(8,128)(2,1)} %param.21) | copy-start | bytes 98308
  43.0 69.9 %copy-start.46 = (bf16[256,64]{0,1:T(8,128)(2,1)S(1)}, bf16[256,64]{0,1:T(8,128)(2,1)}, u32[]{:S(2)}) copy-start(bf16[256,64]{0,1:T(8,128)(2,1)} %param.26) | copy-start | bytes 98308
  43.0 203.2 %reduce-scatter.14.cloned.1.call-start = ((), (), s32[]{:S(2)}) async-start(), calls=%async_computation.12 | async-start | bytes 2359296 | tf_op jit(solution)/shard_map/reduce_scatter | solution.py:175
  43.7 104.4 %copy-start.51 = (f32[128]{0:T(128)}, f32[128]{0:T(128)S(1)}, u32[]{:S(2)}) copy-start(f32[128]{0:T(128)S(1)} %convert_element_type.206) | copy-start | bytes 1540
  44.4 92.2 %copy-start.49 = (f32[128]{0:T(128)}, f32[128]{0:T(128)S(1)}, u32[]{:S(2)}) copy-start(f32[128]{0:T(128)S(1)} %convert_element_type.210) | copy-start | bytes 1540
  66.8 69.6 %copy-start.24 = (bf16[1024,128]{1,0:T(8,128)(2,1)}, bf16[1024,128]{1,0:T(8,128)(2,1)S(1)}, u32[]{:S(2)}) copy-start(bf16[1024,128]{1,0:T(8,128)(2,1)S(1)} %all_gather.42) | copy-start | bytes 786436
  93.7 42.9 %copy-start.11 = (f32[1024,64]{0,1:T(8,128)}, f32[1024,64]{0,1:T(8,128)S(1)}, u32[]{:S(2)}) copy-start(f32[1024,64]{0,1:T(8,128)S(1)} %get-tuple-element.485) | copy-start | bytes 786436
  173.1 77.8 %copy-start.43 = (bf16[64,384]{1,0:T(8,128)(2,1)S(1)}, bf16[64,384]{1,0:T(8,128)(2,1)}, u32[]{:S(2)}) copy-start(bf16[64,384]{1,0:T(8,128)(2,1)} %param.28) | copy-start | bytes 147460
  173.1 102.2 %copy-start.44 = (bf16[64,384]{1,0:T(8,128)(2,1)S(1)}, bf16[64,384]{1,0:T(8,128)(2,1)}, u32[]{:S(2)}) copy-start(bf16[64,384]{1,0:T(8,128)(2,1)} %param.29) | copy-start | bytes 147460
  173.2 145.9 %all-gather.7.cloned.1.call-start = ((), (), s32[]{:S(2)}) async-start(), calls=%async_computation.13 | async-start | bytes 2359296 | tf_op jit(solution)/shard_map/all_gather | solution.py:182
  250.4 113.7 %all-gather.9.cloned.1.call-start = ((), (), s32[]{:S(2)}) async-start(), calls=%async_computation.15 | async-start | bytes 2359296 | tf_op jit(solution)/shard_map/all_gather | solution.py:193
  250.9 195.0 %reduce-scatter.18.cloned.1.call-start = ((), (), s32[]{:S(2)}) async-start(), calls=%async_computation.16 | async-start | bytes 2359296 | tf_op jit(solution)/shard_map/reduce_scatter | solution.py:204
  373.9 72.1 %copy-start.48 = (f32[128]{0:T(128)S(1)}, f32[128]{0:T(128)}, u32[]{:S(2)}) copy-start(f32[128]{0:T(128)} %copy-done.47) | copy-start | bytes 1540
  373.9 73.4 %copy-start.58 = (f32[128]{0:T(128)S(1)}, f32[128]{0:T(128)}, u32[]{:S(2)}) copy-start(f32[128]{0:T(128)} %copy-done.57) | copy-start | bytes 1540
  373.9 129.5 %all-gather.11.cloned.1.call-start = ((), (), s32[]{:S(2)}) async-start(), calls=%async_computation.17 | async-start | bytes 2359296 | tf_op jit(solution)/shard_map/all_gather | solution.py:213
  449.4 112.4 %reduce-scatter.34.cloned.1.call-start = ((), (), s32[]{:S(2)}) async-start(), calls=%async_computation.25 | async-start | bytes 835584
  455.5 168.0 %reduce-scatter.32.cloned.1.call-start = ((), (), s32[]{:S(2)}) async-start(), calls=%async_computation.24 | async-start | bytes 835584 | tf_op jit(solution)/shard_map/reduce_scatter | solution.py:306
  459.6 226.1 %reduce-scatter.30.cloned.1.call-start = ((), (), s32[]{:S(2)}) async-start(), calls=%async_computation.23 | async-start | bytes 835584 | tf_op jit(solution)/shard_map/reduce_scatter | solution.py:303
  463.7 283.5 %reduce-scatter.24.cloned.1.call-start = ((), (), s32[]{:S(2)}) async-start(), calls=%async_computation.20 | async-start | bytes 278528 | tf_op jit(solution)/shard_map/reduce_scatter | solution.py:297
  542.0 266.1 %reduce-scatter.26.cloned.1.call-start = ((), (), s32[]{:S(2)}) async-start(), calls=%async_computation.21 | async-start | bytes 278528 | tf_op jit(solution)/shard_map/reduce_scatter | solution.py:300
  545.6 323.8 %reduce-scatter.22.cloned.1.call-start = ((), (), s32[]{:S(2)}) async-start(), calls=%async_computation.19 | async-start | bytes 557056 | tf_op jit(solution)/shard_map/reduce_scatter | solution.py:294
  550.0 380.9 %reduce-scatter.28.cloned.1.call-start = ((), (), s32[]{:S(2)}) async-start(), calls=%async_computation.22 | async-start | bytes 557056 | tf_op jit(solution)/shard_map/reduce_scatter | solution.py:309
  553.3 457.5 %reduce-scatter.20.cloned.1.call-start = ((), (), s32[]{:S(2)}) async-start(), calls=%async_computation.18 | async-start | bytes 2359296 | tf_op jit(solution)/shard_map/reduce_scatter | solution.py:273
  557.8 531.3 %reduce-scatter.16.cloned.1.call-start = ((), (), s32[]{:S(2)}) async-start(), calls=%async_computation.14 | async-start | bytes 2359296 | tf_op jit(solution)/shard_map/reduce_scatter | solution.py:186
  561.7 449.2 %copy-start.4 = (bf16[128,1024]{1,0:T(8,128)(2,1)S(1)}, bf16[128,1024]{1,0:T(8,128)(2,1)}, u32[]{:S(2)}) copy-start(bf16[128,1024]{1,0:T(8,128)(2,1)} %param.18) | copy-start | bytes 786436
  561.7 449.2 %copy-start.42 = (f32[1024]{0:T(1024)S(1)}, f32[1024]{0:T(1024)}, u32[]{:S(2)}) copy-start(f32[1024]{0:T(1024)} %copy-done.41) | copy-start | bytes 12292
  561.7 449.2 %copy-start.54 = (f32[128]{0:T(128)S(1)}, f32[128]{0:T(128)}, u32[]{:S(2)}) copy-start(f32[128]{0:T(128)} %copy-done.53) | copy-start | bytes 1540
  561.7 519.0 %copy-start.56 = (f32[128]{0:T(128)S(1)}, f32[128]{0:T(128)}, u32[]{:S(2)}) copy-start(f32[128]{0:T(128)} %copy-done.55) | copy-start | bytes 1540
  561.7 527.3 %copy-start.9 = (bf16[128,1024]{1,0:T(8,128)(2,1)S(1)}, bf16[128,1024]{1,0:T(8,128)(2,1)}, u32[]{:S(2)}) copy-start(bf16[128,1024]{1,0:T(8,128)(2,1)} %reduce-scatter.14.cloned.1.call-done) | copy-start | bytes 786436
  561.7 527.3 %copy-start.22 = (bf16[128,1024]{1,0:T(8,128)(2,1)S(1)}, bf16[128,1024]{1,0:T(8,128)(2,1)}, u32[]{:S(2)}) copy-start(bf16[128,1024]{1,0:T(8,128)(2,1)} %param.31) | copy-start | bytes 786436
  561.7 527.3 %copy-start.23 = (bf16[128,1024]{1,0:T(8,128)(2,1)S(1)}, bf16[128,1024]{1,0:T(8,128)(2,1)}, u32[]{:S(2)}) copy-start(bf16[128,1024]{1,0:T(8,128)(2,1)} %reduce-scatter.18.cloned.1.call-done) | copy-start | bytes 786436
  (54 other events, 175.3 us)
Sparse Core Ops, SparseCore 0:
  43.1 57.5 all-gather.4
  173.3 72.9 reduce-scatter.13
  250.5 57.4 all-gather.6
  310.2 53.7 all-gather.8
  374.0 71.8 reduce-scatter.17
  449.5 53.8 all-gather.10
  505.8 55.5 reduce-scatter.33
  563.9 59.6 reduce-scatter.31
  625.9 59.6 reduce-scatter.29
  688.5 58.6 reduce-scatter.23
  749.5 58.4 reduce-scatter.25
  810.4 58.9 reduce-scatter.21
  871.7 59.1 reduce-scatter.27
  934.9 75.8 reduce-scatter.19
  1014.9 74.0 reduce-scatter.15
where the time goes:
time: 1100 us
  waiting for transfers between devices  670 us (61%)
  blocking collectives  246 us (22%)
  matrix products  74.8 us (7%)
  other arithmetic  56.6 us (5%)
  local copies, waits for them, and re-layouts  34.1 us (3%)
  between operations  15.5 us (1%)
    reduce_scatter x1, waiting for transfers between devices, per_device(): lax.psum_scatter((rows_times(grad_query_pre, query_full) + rows_times(gra...  78.6 us
    reduce_scatter x1, waiting for transfers between devices, per_device(): lax.psum_scatter(rows_times(mixed_out, out_full).astype(jnp.bfloat16), 't...  72.4 us
    reduce_scatter x1, waiting for transfers between devices, per_device(): lax.psum_scatter((rows_times(grad_gate, gate_full) + rows_times(grad_up,...  72 us
    psum x1, blocking collectives, per_device(): lax.psum((grad_gain_one, grad_gain_two, grad_gain_query, grad_gain_key),...  67.5 us
    reduce_scatter x1, waiting for transfers between devices, per_device(): lax.psum_scatter(grad_gate_full.astype(jnp.bfloat16), 'dp', scatter_dimen...  60.6 us
    reduce_scatter x1, waiting for transfers between devices, per_device(): lax.psum_scatter(grad_out_full.astype(jnp.bfloat16), 'dp', scatter_dimens...  60.1 us
    reduce_scatter x1, waiting for transfers between devices, per_device(): lax.psum_scatter(grad_key_full.astype(jnp.bfloat16), 'dp', scatter_dimens...  60.1 us
    reduce_scatter x1, waiting for transfers between devices, per_device(): lax.psum_scatter(grad_query_full.astype(jnp.bfloat16), 'dp', scatter_dime...  60 us
  transfers between devices with their start and end apart: 15, of which 12 were waited for; matrix products, arithmetic and copies ran while one was open for 9% of the time, Pallas kernels for 0%

commit v1 on v0

v1 whole, which is shorter than its diff:
```python
import functools

import jax
import jax.numpy as jnp
from jax import lax
from jax.experimental import pallas as pl
from jax.experimental.pallas import tpu as pltpu
from jax.sharding import PartitionSpec as P

MESH = pl.DeviceIdType.MESH
BF = jnp.bfloat16
F32 = jnp.float32
HEAD = 128
EPS = 1e-06
ROPE_BASE = 1000000.0
MASKED = -1e30
SCALE = HEAD ** (-0.5)
TOK = 128
GROUP = 1024
WIDTH = 1024
NA = 768
NM = 1152
CH = 256
N_SEMS = 220


def dot(a, b):
    return jnp.dot(a, b, preferred_element_type=F32)


def dot_nt(a, b):
    return lax.dot_general(a, b, (((1,), (1,)), ((), ())), preferred_element_type=F32)


def dot_tn(a, b):
    return lax.dot_general(a, b, (((0,), (0,)), ((), ())), preferred_element_type=F32)


class Links:
    def __init__(self, send_sems, recv_sems):
        self.send_sems, self.recv_sems = send_sems, recv_sems
        self.sends, self.recvs = 0, 0
        self.pending = []

    def send_ids(self, count=1):
        first = self.sends
        self.sends += count
        assert self.sends <= N_SEMS
        return first

    def recv_ids(self, count=1):
        first = self.recvs
        self.recvs += count
        assert self.recvs <= N_SEMS
        return first

    def copy(self, src, dst, device, send_id, recv_id):
        return pltpu.make_async_remote_copy(
            src_ref=src,
            dst_ref=dst,
            send_sem=self.send_sems.at[send_id],
            recv_sem=self.recv_sems.at[recv_id],
            device_id=device,
            device_id_type=MESH,
        )

    def send(self, src, dst, device, recv_id):
        copy = self.copy(src, dst, device, self.send_ids(), recv_id)
        copy.start()
        self.pending.append(copy)

    def wait(self, dst, device, recv_id):
        self.copy(dst, dst, device, 0, recv_id).wait_recv()

    def drain(self):
        for copy in self.pending:
            copy.wait_send()


class Place:
    def __init__(self):
        self.d = lax.axis_index("dp")
        self.t = lax.axis_index("tensor")
        self.x = self.d // 4
        self.y = (self.d // 2) % 2
        self.c = self.d % 2

    def dp_index(self, dx, dy, dc):
        return ((self.x + dx) % 4) * 4 + ((self.y + dy) % 2) * 2 + (self.c + dc) % 2

    def dp_peer(self, dx, dy, dc):
        return (self.dp_index(dx, dy, dc), self.t)

    def tensor_peer(self, t):
        return (self.d, t)


class WeightGather:
    def __init__(self, links, place, buf):
        self.links, self.place, self.buf = links, place, buf
        names = ["y", "xm0", "xp0", "xm1", "xp1", "l0", "r0", "l1", "r1"]
        names += ["c%d%d" % (dx, dy) for dx in range(4) for dy in range(2)]
        self.ids = {name: links.recv_ids() for name in names}

    def rows(self, dx, dy, dc, half=None):
        first = self.place.dp_index(dx, dy, dc) * 64
        if half is None:
            return self.buf.at[pl.ds(pl.multiple_of(first, 64), 64)]
        return self.buf.at[pl.ds(pl.multiple_of(first + 32 * half, 32), 32)]

    def push(self, src, dst, device, name):
        self.links.send(src, dst, device, self.ids[name])

    def core(self, dx, dy):
        ref = self.rows(dx, dy, 0)
        self.push(ref, ref, self.place.dp_peer(0, 0, 1), "c%d%d" % (dx, dy))

    def got(self, ref, device, name):
        self.links.wait(ref, device, self.ids[name])

    def begin(self):
        place, own = self.place, self.rows(0, 0, 0)
        self.push(own, own, place.dp_peer(0, 1, 0), "y")
        self.push(own, own, place.dp_peer(1, 0, 0), "xm0")
        self.push(own, own, place.dp_peer(3, 0, 0), "xp0")
        self.core(0, 0)

    def second(self):
        place, ref = self.place, self.rows(0, 1, 0)
        self.got(ref, place.dp_peer(0, 1, 0), "y")
        self.push(ref, ref, place.dp_peer(1, 0, 0), "xm1")
        self.push(ref, ref, place.dp_peer(3, 0, 0), "xp1")
        self.core(0, 1)

    def third(self, dy):
        place = self.place
        left, right = place.dp_peer(3, 0, 0), place.dp_peer(1, 0, 0)
        self.got(self.rows(3, dy, 0), left, "xm%d" % dy)
        half = self.rows(3, dy, 0, 0)
        self.push(half, half, right, "l%d" % dy)
        self.got(self.rows(1, dy, 0), right, "xp%d" % dy)
        half = self.rows(1, dy, 0, 1)
        self.push(half, half, left, "r%d" % dy)
        self.core(3, dy)
        self.core(1, dy)

    def fourth(self, dy):
        place = self.place
        self.got(self.rows(2, dy, 0, 0), place.dp_peer(3, 0, 0), "l%d" % dy)
        self.got(self.rows(2, dy, 0, 1), place.dp_peer(1, 0, 0), "r%d" % dy)
        self.core(2, dy)

    def finish(self):
        for dx in range(4):
            for dy in range(2):
                self.got(self.rows(dx, dy, 1), self.place.dp_peer(0, 0, 1), "c%d%d" % (dx, dy))


class WeightSum:
    def __init__(self, links, place, full, core_in, total, side, last, wide):
        self.links, self.place, self.full = links, place, full
        self.core_in, self.total, self.side, self.last, self.wide = core_in, total, side, last, wide
        self.ids = {n: links.recv_ids() for n in ("core", "la", "lr", "ra", "rr", "lc", "rc", "y")}

    def begin(self):
        place = self.place
        self.links.send(self.full.at[:, (place.c + 1) % 2], self.core_in, place.dp_peer(0, 0, 1), self.ids["core"])

    def cross(self):
        place, links, side = self.place, self.links, self.side
        links.wait(self.core_in, place.dp_peer(0, 0, 1), self.ids["core"])

        def add(i, carry):
            self.total[i] = (
                self.full[i, place.c].astype(F32) + self.core_in[i].astype(F32)
            ).astype(BF)
            return carry

        lax.fori_loop(0, 8, add, 0)
        left, right = place.dp_peer(3, 0, 0), place.dp_peer(1, 0, 0)
        x = place.x
        links.send(self.total.at[((x + 2) % 4) * 2], side.at[0], right, self.ids["la"])
        links.send(self.total.at[((x + 2) % 4) * 2 + 1], side.at[2], left, self.ids["ra"])
        links.send(self.total.at[((x + 1) % 4) * 2 + 1], side.at[1], right, self.ids["lr"])
        links.send(self.total.at[((x + 3) % 4) * 2], side.at[3], left, self.ids["rr"])

    def relay(self):
        place, links, side = self.place, self.links, self.side
        left, right = place.dp_peer(3, 0, 0), place.dp_peer(1, 0, 0)
        x = place.x
        links.wait(side.at[0], left, self.ids["la"])
        side[7] = (self.total[((x + 1) % 4) * 2].astype(F32) + side[0].astype(F32)).astype(BF)
        links.send(side.at[7], side.at[4], right, self.ids["lc"])
        links.wait(side.at[2], right, self.ids["ra"])
        side[8] = (self.total[((x + 3) % 4) * 2 + 1].astype(F32) + side[2].astype(F32)).astype(BF)
        links.send(side.at[8], side.at[5], left, self.ids["rc"])

    def pair(self):
        place, links, side = self.place, self.links, self.side
        left, right = place.dp_peer(3, 0, 0), place.dp_peer(1, 0, 0)
        links.wait(side.at[1], left, self.ids["lr"])
        links.wait(side.at[3], right, self.ids["rr"])
        links.wait(side.at[4], left, self.ids["lc"])
        links.wait(side.at[5], right, self.ids["rc"])
        x = place.x
        self.wide[0] = self.total[x * 2].astype(F32) + side[4].astype(F32) + side[3].astype(F32)
        self.wide[1] = self.total[x * 2 + 1].astype(F32) + side[5].astype(F32) + side[1].astype(F32)
        side[9] = self.wide[(place.y + 1) % 2].astype(BF)
        links.send(side.at[9], side.at[6], place.dp_peer(0, 1, 0), self.ids["y"])

    def finish(self):
        place = self.place
        self.links.wait(self.side.at[6], place.dp_peer(0, 1, 0), self.ids["y"])
        self.last[...] = self.wide[place.y] + self.side[6].astype(F32)


class TokenSum:
    def __init__(self, links, place, partial, landed):
        self.links, self.place, self.partial, self.landed = links, place, partial, landed
        self.send_id, self.recv_id = links.send_ids(8), links.recv_ids(8)

    def copy_to(self, t):
        rows = pl.ds(pl.multiple_of(t * TOK, TOK), TOK)
        me = self.place.t
        return self.links.copy(
            self.partial.at[rows], self.landed.at[me], self.place.tensor_peer(t), self.send_id + t, self.recv_id + me
        )

    def send_block(self, t):
        @pl.when(t != self.place.t)
        def _():
            self.copy_to(t).start()

    def total(self):
        place, links = self.place, self.links
        own = pl.ds(pl.multiple_of(place.t * TOK, TOK), TOK)
        acc = self.partial[own].astype(F32)
        for k in range(1, 8):
            src = (place.t + k) % 8
            links.wait(self.landed.at[src], place.tensor_peer(src), self.recv_id + src)
        for k in range(1, 8):
            acc = acc + self.landed[(place.t + k) % 8].astype(F32)
        return acc

    def drain(self):
        for k in range(1, 8):
            self.copy_to((self.place.t + k) % 8).wait_send()


class TokenGather:
    def __init__(self, links, place, buf):
        self.links, self.place, self.buf = links, place, buf
        self.recv_id = links.recv_ids(8)

    def rows(self, t):
        return self.buf.at[pl.ds(pl.multiple_of(t * TOK, TOK), TOK)]

    def begin(self):
        t = self.place.t
        order = [t + 1 - 2 * (t % 2)]
        for k in range(1, 4):
            first = ((t // 2 + 4 - k) % 4) * 2
            order += [first + t % 2, first + 1 - t % 2]
        own = self.rows(t)
        for peer in order:
            self.links.send(own, own, self.place.tensor_peer(peer), self.recv_id + t)

    def wait(self, t):
        self.links.wait(self.rows(t), self.place.tensor_peer(t), self.recv_id + t)

    def wait_all(self):
        for k in range(1, 8):
            self.wait((self.place.t + k) % 8)


def layer_kernel(
    wa_own,
    wm_own,
    gain_own,
    x_own,
    og_own,
    query_gain,
    key_gain,
    cosine,
    sine,
    starts,
    out_ref,
    in_grad_ref,
    ga_ref,
    gm_ref,
    gains_ref,
    wa,
    wm,
    gain_in,
    gain_one,
    gain_two,
    xs,
    ogs,
    h1,
    r1,
    qk_pre,
    q_rot,
    k_rot,
    vals,
    mixed,
    lse,
    p1,
    l1,
    middle,
    h2,
    grad_act,
    act,
    dgu,
    p2,
    l2,
    po,
    lo,
    gb,
    grad_mid,
    dk,
    dv,
    dqkv,
    p3,
    l3,
    gm_full,
    gm_core,
    gm_total,
    gm_side,
    gm_wide,
    ga_full,
    ga_core,
    ga_total,
    ga_side,
    ga_wide,
    gg,
    gg_sum,
    gg_t,
    gg_d,
    send_sems,
    recv_sems,
):
    links = Links(send_sems, recv_sems)
    place = Place()
    d, t = place.d, place.t
    own = pl.ds(pl.multiple_of(t * TOK, TOK), TOK)
    own_w = pl.ds(pl.multiple_of(d * 64, 64), 64)
    dp_peers = [(k // 4, (k // 2) % 2, k % 2) for k in range(1, 16)]

    barrier = pltpu.get_barrier_semaphore()
    for k in range(1, 8):
        pl.semaphore_signal(
            barrier, inc=1, device_id=place.tensor_peer((t + k) % 8), device_id_type=MESH
        )
    for k in dp_peers:
        pl.semaphore_signal(barrier, inc=1, device_id=place.dp_peer(*k), device_id_type=MESH)

    xs[own] = x_own[...]
    ogs[own] = og_own[...]
    wa[own_w] = wa_own[...]
    wm[own_w] = wm_own[...]
    gain_in[d] = gain_own[...]

    pl.semaphore_wait(barrier, 22)

    gather_a = WeightGather(links, place, wa)
    gather_m = WeightGather(links, place, wm)
    gather_x = TokenGather(links, place, xs)
    gather_og = TokenGather(links, place, ogs)
    gather_h2 = TokenGather(links, place, h2)
    gather_gb = TokenGather(links, place, gb)
    sum_1 = TokenSum(links, place, p1, l1)
    sum_2 = TokenSum(links, place, p2, l2)
    sum_o = TokenSum(links, place, po, lo)
    sum_3 = TokenSum(links, place, p3, l3)
    weight_m = WeightSum(links, place, gm_full, gm_core, gm_total, gm_side, gm_ref, gm_wide)
    weight_a = WeightSum(links, place, ga_full, ga_core, ga_total, ga_side, ga_ref, ga_wide)

    gather_a.begin()
    gain_id = links.recv_ids(16)
    for k in dp_peers:
        links.send(gain_in.at[d], gain_in.at[d], place.dp_peer(*k), gain_id + d)
    gather_x.begin()
    gather_a.second()
    gather_a.third(0)
    gather_a.third(1)
    gather_m.begin()

    for k in dp_peers:
        src = place.dp_index(*k)
        links.wait(gain_in.at[src], place.dp_peer(*k), gain_id + src)
    low = lax.broadcasted_iota(jnp.int32, (1, 128), 1) < 64
    for k in range(8):
        even, odd = gain_in[2 * k][0:1], gain_in[2 * k + 1][0:1]
        cols = slice(128 * k, 128 * k + 128)
        gain_one[0:1, cols] = jnp.where(low, even, pltpu.roll(odd, 64, 1))
        gain_two[0:1, cols] = jnp.where(low, pltpu.roll(even, 64, 1), odd)

    gather_a.fourth(0)
    gather_a.fourth(1)
    gather_x.wait_all()

    def norm_chunk(i, carry):
        rows = pl.ds(pl.multiple_of(i * 128, 128), 128)
        wide = xs[rows].astype(F32)
        r = lax.rsqrt(jnp.mean(wide * wide, axis=-1, keepdims=True) + EPS)
        r1[rows] = r
        h1[rows] = (wide * r * gain_one[0:1]).astype(BF)
        return carry

    lax.fori_loop(0, 8, norm_chunk, 0)
    gather_a.finish()
    gather_og.begin()
    gather_m.second()

    def qkv_chunk(i, carry):
        rows = pl.ds(pl.multiple_of(i * CH, CH), CH)
        pre = dot(h1[rows], wa[:, 0:512])
        qk_pre[rows] = pre[:, 0:384]
        vals[rows] = pre[:, 384:512].astype(BF)
        cos, sin = cosine[rows], sine[rows]
        for h in range(3):
            part = pre[:, 128 * h : 128 * h + 128]
            r = lax.rsqrt(jnp.mean(part * part, axis=-1, keepdims=True) + EPS)
            scaled = part * r * (query_gain if h < 2 else key_gain)[0:1]
            turned = (scaled * cos + pltpu.roll(scaled, 64, 1) * sin).astype(BF)
            if h < 2:
                q_rot[h, rows] = turned
            else:
                k_rot[rows] = turned
        return carry

    lax.fori_loop(0, 4, qkv_chunk, 0)
    gather_m.third(0)
    gather_m.third(1)

    def allowed(qb, keys):
        key_at = lax.broadcasted_iota(jnp.int32, (CH, keys), 1)
        query_at = lax.broadcasted_iota(jnp.int32, (CH, keys), 0) + qb * CH
        return (key_at >= starts[qb * CH : qb * CH + CH]) & (key_at <= query_at)

    for qb in range(4):
        rows = slice(qb * CH, qb * CH + CH)
        keys = CH * (qb + 1)
        ok = allowed(qb, keys)
        for h in range(2):
            scores = jnp.where(ok, dot_nt(q_rot[h, rows], k_rot[0:keys]) * SCALE, MASKED)
            top = jnp.max(scores, axis=-1, keepdims=True)
            terms = jnp.exp(scores - top)
            total = jnp.sum(terms, axis=-1, keepdims=True)
            lse[h, rows] = top + jnp.log(total)
            weights = (terms * (1.0 / total)).astype(BF)
            mixed[rows, 128 * h : 128 * h + 128] = dot(weights, vals[0:keys]).astype(BF)
        p1[rows] = dot_nt(mixed[rows], wa[:, 512:768]).astype(BF)
        sum_1.send_block(2 * qb)
        sum_1.send_block(2 * qb + 1)

    gather_m.fourth(0)
    gather_m.fourth(1)
    gather_og.wait_all()
    gather_m.finish()

    def grad_act_chunk(i, carry):
        rows = pl.ds(pl.multiple_of(i * CH, CH), CH)
        grad_act[rows] = dot(ogs[rows], wm[:, 768:1152])
        return carry

    lax.fori_loop(0, 4, grad_act_chunk, 0)

    mid = x_own[...].astype(F32) + sum_1.total()
    middle[...] = mid
    r_two = lax.rsqrt(jnp.mean(mid * mid, axis=-1, keepdims=True) + EPS)
    h2[own] = (mid * r_two * gain_two[0:1]).astype(BF)
    gather_h2.begin()

    def mlp_chunk(j):
        rows = pl.ds(pl.multiple_of(j * CH, CH), CH)
        pre = dot(h2[rows], wm[:, 0:768])
        gate, up = pre[:, 0:384], pre[:, 384:768]
        sig = 1.0 / (1.0 + jnp.exp(-gate))
        silu = gate * sig
        acted = (silu * up).astype(BF)
        act[rows] = acted
        grad = grad_act[rows]
        dgu[rows, 0:384] = (grad * up * (sig * (1.0 + gate * (1.0 - sig)))).astype(BF)
        dgu[rows, 384:768] = (grad * silu).astype(BF)
        p2[rows] = dot_nt(dgu[rows], wm[:, 0:768]).astype(BF)
        sum_2.send_block(2 * j)
        sum_2.send_block(2 * j + 1)
        po[rows] = dot_nt(acted, wm[:, 768:1152]).astype(BF)

    gather_h2.wait(t + 1 - 2 * (t % 2))
    mlp_chunk(t // 2)

    def mlp_step(k, carry):
        j = (t // 2 + k) % 4
        gather_h2.wait(2 * j)
        gather_h2.wait(2 * j + 1)
        mlp_chunk(j)
        return carry

    lax.fori_loop(1, 4, mlp_step, 0)
    for k in range(1, 8):
        sum_o.send_block((t + k) % 8)

    def mlp_weight_chunk(i, carry):
        cols = pl.ds(pl.multiple_of(i * CH, CH), CH)
        pair = pl.ds(i * 2, 2)
        gm_full[pair, :, :, 0:768] = dot_tn(h2[:, cols], dgu[...]).astype(BF).reshape(2, 2, 64, 768)
        gm_full[pair, :, :, 768:1152] = dot_tn(ogs[:, cols], act[...]).astype(BF).reshape(2, 2, 64, 384)
        return carry

    lax.fori_loop(0, 4, mlp_weight_chunk, 0)
    weight_m.begin()

    err = sum_2.total()
    mid = middle[...]
    r_two = lax.rsqrt(jnp.mean(mid * mid, axis=-1, keepdims=True) + EPS)
    normed = mid * r_two
    part = jnp.sum(err * normed, axis=0, keepdims=True)
    gg[...] = jnp.zeros_like(gg)
    for k in range(8):
        gg[8 + k : 9 + k] = part[:, 128 * k : 128 * k + 128]
    scaled = err * gain_two[0:1]
    grad = og_own[...].astype(F32) + r_two * (
        scaled - normed * jnp.mean(scaled * normed, axis=-1, keepdims=True)
    )
    grad_mid[...] = grad
    gb[own] = grad.astype(BF)
    gather_gb.begin()
    weight_m.cross()

    out_ref[...] = (middle[...] + sum_o.total()).astype(BF)
    dk[...] = jnp.zeros_like(dk)
    dv[...] = jnp.zeros_like(dv)
    gather_gb.wait_all()

    def back_rope(turned, pre, gain, cos, sin):
        r = lax.rsqrt(jnp.mean(pre * pre, axis=-1, keepdims=True) + EPS)
        normed = pre * r
        err = turned * cos - pltpu.roll(turned, 64, 1) * sin
        scaled = err * gain
        grad = r * (scaled - normed * jnp.mean(scaled * normed, axis=-1, keepdims=True))
        return grad, jnp.sum(err * normed, axis=0, keepdims=True)

    attn_part = jnp.zeros((1, WIDTH), F32)
    for qb in (3, 2, 1, 0):
        rows = slice(qb * CH, qb * CH + CH)
        keys = CH * (qb + 1)
        ok = allowed(qb, keys)
        cos, sin = cosine[rows], sine[rows]
        grad_mixed = dot(gb[rows], wa[:, 512:768]).astype(BF)
        for h in range(2):
            grad_h = grad_mixed[:, 128 * h : 128 * h + 128]
            scores = jnp.where(ok, dot_nt(q_rot[h, rows], k_rot[0:keys]) * SCALE, MASKED)
            probs = jnp.exp(scores - lse[h, rows])
            grad_probs = dot_nt(grad_h, vals[0:keys])
            inner = jnp.sum(probs * grad_probs, axis=-1, keepdims=True)
            grad_scores = (probs * (grad_probs - inner)).astype(BF)
            dk[0:keys] += dot_tn(grad_scores, q_rot[h, rows]) * SCALE
            dv[0:keys] += dot_tn(probs.astype(BF), grad_h)
            grad_q = (dot(grad_scores, k_rot[0:keys]) * SCALE).astype(BF).astype(F32)
            pre = qk_pre[rows, 128 * h : 128 * h + 128]
            grad, gain_part = back_rope(grad_q, pre, query_gain[0:1], cos, sin)
            dqkv[rows, 128 * h : 128 * h + 128] = grad.astype(BF)
            gg[16:17] += gain_part
        grad_k = dk[rows].astype(BF).astype(F32)
        grad, gain_part = back_rope(grad_k, qk_pre[rows, 256:384], key_gain[0:1], cos, sin)
        dqkv[rows, 256:384] = grad.astype(BF)
        gg[17:18] += gain_part
        dqkv[rows, 384:512] = dv[rows].astype(BF)
        err = dot_nt(dqkv[rows], wa[:, 0:512])
        p3[rows] = err.astype(BF)
        sum_3.send_block(2 * qb)
        sum_3.send_block(2 * qb + 1)
        attn_part += jnp.sum(err * (xs[rows].astype(F32) * r1[rows]), axis=0, keepdims=True)
        if qb == 2:
            weight_m.relay()
        if qb == 0:
            weight_m.pair()

    for k in range(8):
        gg[k : k + 1] = attn_part[:, 128 * k : 128 * k + 128]
    gg_id = links.recv_ids(8)
    for k in range(1, 8):
        links.send(gg, gg_t.at[t], place.tensor_peer((t + k) % 8), gg_id + t)

    def attn_weight_chunk(i, carry):
        cols = pl.ds(pl.multiple_of(i * CH, CH), CH)
        pair = pl.ds(i * 2, 2)
        ga_full[pair, :, :, 0:512] = dot_tn(h1[:, cols], dqkv[...]).astype(BF).reshape(2, 2, 64, 512)
        ga_full[pair, :, :, 512:768] = dot_tn(gb[:, cols], mixed[...]).astype(BF).reshape(2, 2, 64, 256)
        return carry

    lax.fori_loop(0, 4, attn_weight_chunk, 0)
    weight_a.begin()

    total = gg[...]
    for k in range(1, 8):
        src = (t + k) % 8
        links.wait(gg_t.at[src], place.tensor_peer(src), gg_id + src)
        total = total + gg_t[src]
    gg_sum[...] = total
    gg_id2 = links.recv_ids(16)
    for k in dp_peers:
        links.send(gg_sum, gg_d.at[d], place.dp_peer(*k), gg_id2 + d)

    weight_a.cross()
    weight_m.finish()
    weight_a.relay()

    gg_d[d] = gg_sum[...]
    for k in dp_peers:
        src = place.dp_index(*k)
        links.wait(gg_d.at[src], place.dp_peer(*k), gg_id2 + src)
    total = gg_d[0]
    for k in range(1, 16):
        total = total + gg_d[k]
    gains_ref[...] = total

    weight_a.pair()
    err = sum_3.total()
    r_one = r1[own]
    normed = x_own[...].astype(F32) * r_one
    scaled = err * gain_one[0:1]
    in_grad_ref[...] = (
        grad_mid[...]
        + r_one * (scaled - normed * jnp.mean(scaled * normed, axis=-1, keepdims=True))
    ).astype(BF)
    weight_a.finish()

    links.drain()
    for each in (sum_1, sum_2, sum_o, sum_3):
        each.drain()


def run_layer(*args):
    vmem = pl.BlockSpec(memory_space=pltpu.VMEM)

    def sds(shape, kind):
        return jax.ShapeDtypeStruct(shape, kind)

    def buf(shape, kind=BF):
        return pltpu.VMEM(shape, kind)

    group = (GROUP, WIDTH)
    landing = (8, TOK, WIDTH)
    scratch = [
        buf((WIDTH, NA)),
        buf((WIDTH, NM)),
        buf((16, 8, 128), F32),
        buf((1, WIDTH), F32),
        buf((1, WIDTH), F32),
        buf(group),
        buf(group),
        buf(group),
        buf((GROUP, 1), F32),
        buf((GROUP, 384), F32),
        buf((2, GROUP, HEAD)),
        buf((GROUP, HEAD)),
        buf((GROUP, HEAD)),
        buf((GROUP, 256)),
        buf((2, GROUP, 1), F32),
        buf(group),
        buf(landing),
        buf((TOK, WIDTH), F32),
        buf(group),
        buf((GROUP, 384), F32),
        buf((GROUP, 384)),
        buf((GROUP, 768)),
        buf(group),
        buf(landing),
        buf(group),
        buf(landing),
        buf(group),
        buf((TOK, WIDTH), F32),
        buf((GROUP, HEAD), F32),
        buf((GROUP, HEAD), F32),
        buf((GROUP, 512)),
        buf(group),
        buf(landing),
        buf((8, 2, 64, NM)),
        buf((8, 64, NM)),
        buf((8, 64, NM)),
        buf((10, 64, NM)),
        buf((2, 64, NM), F32),
        buf((8, 2, 64, NA)),
        buf((8, 64, NA)),
        buf((8, 64, NA)),
        buf((10, 64, NA)),
        buf((2, 64, NA), F32),
        buf((24, 128), F32),
        buf((24, 128), F32),
        buf((8, 24, 128), F32),
        buf((16, 24, 128), F32),
        pltpu.SemaphoreType.DMA((N_SEMS,)),
        pltpu.SemaphoreType.DMA((N_SEMS,)),
    ]
    return pl.pallas_call(
        layer_kernel,
        out_shape=(
            sds((TOK, WIDTH), BF),
            sds((TOK, WIDTH), BF),
            sds((64, NA), F32),
            sds((64, NM), F32),
            sds((24, 128), F32),
        ),
        in_specs=[vmem] * len(args),
        out_specs=(vmem,) * 5,
        scratch_shapes=scratch,
        name="layer",
        compiler_params=pltpu.CompilerParams(
            collective_id=0, has_side_effects=True, vmem_limit_bytes=63 * 2**20
        ),
    )(*args)


def tables(lengths):
    ends = jnp.cumsum(lengths)
    begins = ends - lengths
    at = jnp.arange(GROUP, dtype=jnp.int32)
    label = jnp.sum((at[:, None] >= ends[None, :]).astype(jnp.int32), axis=1)
    chosen = label[:, None] == jnp.arange(lengths.shape[0], dtype=jnp.int32)[None, :]
    starts = jnp.sum(jnp.where(chosen, begins[None, :], 0), axis=1)
    half = HEAD // 2
    frequency = ROPE_BASE ** (-(jnp.arange(half).astype(F32) * 2.0 / HEAD))
    angles = (at - starts).astype(F32)[:, None] * frequency[None, :]
    cos, sin = jnp.cos(angles), jnp.sin(angles)
    return (
        jnp.concatenate([cos, cos], axis=-1),
        jnp.concatenate([-sin, sin], axis=-1),
        starts[:, None],
    )


def per_device(
    layer_input,
    seq_lengths,
    attn_gain,
    w_query,
    key_projection,
    value_projection,
    query_gain,
    key_gain,
    w_out,
    mlp_gain,
    w_gate,
    w_up,
    w_down,
    out_grad,
):
    cosine, sine, starts = tables(seq_lengths[0])
    wa_own = jnp.concatenate([w_query, key_projection, value_projection, w_out.T], axis=1)
    wm_own = jnp.concatenate([w_gate, w_up, w_down.T], axis=1)
    gain_own = jnp.broadcast_to(jnp.concatenate([attn_gain, mlp_gain]).astype(F32)[None], (8, 128))
    out, in_grad, ga, gm, gains = run_layer(
        wa_own,
        wm_own,
        gain_own,
        layer_input,
        out_grad,
        query_gain.astype(F32)[None],
        key_gain.astype(F32)[None],
        cosine,
        sine,
        starts,
    )
    piece = attn_gain.shape[0]
    first = lax.axis_index("dp") * piece
    grad_attn_gain = lax.dynamic_slice_in_dim(gains[0:8].reshape(-1), first, piece, 0)
    grad_mlp_gain = lax.dynamic_slice_in_dim(gains[8:16].reshape(-1), first, piece, 0)
    return (
        out,
        in_grad,
        grad_attn_gain,
        ga[:, 0:256],
        ga[:, 256:384],
        ga[:, 384:512],
        gains[16],
        gains[17],
        ga[:, 512:768].T,
        grad_mlp_gain,
        gm[:, 0:384],
        gm[:, 384:768],
        gm[:, 768:1152].T,
    )


def solution(mesh):
    both = P(("dp", "tensor"), None)
    split = P("dp", "tensor")
    turned = P("tensor", "dp")
    in_specs = (
        both,
        P("dp", None),
        P("dp"),
        split,
        split,
        split,
        P(),
        P(),
        turned,
        P("dp"),
        split,
        split,
        turned,
        both,
    )
    out_specs = (both, both, P("dp"), split, split, split, P(), P(), turned, P("dp"), split, split, turned)
    return jax.shard_map(
        per_device, mesh=mesh, in_specs=in_specs, out_specs=out_specs, check_vma=False
    )
```

time: 1100 us -> 287 us (0.26)
  waiting for transfers between devices: 670 us -> 0 us
  Pallas kernels: 0 us -> 267 us
  blocking collectives: 246 us -> 0 us
  matrix products: 74.8 us -> 0 us
  other arithmetic: 56.6 us -> 5.5 us
  local copies, waits for them, and re-layouts: 34.1 us -> 10.3 us
  between operations: 15.5 us -> 0.76 us
    reduce_scatter x10 -> x0, waiting for transfers between devices: 592 us -> none  [the longest x1 78.6 us: per_device(): lax.psum_scatter((rows_times(grad_query_pre, query_full) + rows_times(gra...]
    pallas_call x0 -> x1, Pallas kernels: none -> 267 us  [run_layer(): pl.pallas_call(layer_kernel, out_shape=(sds((TOK, WIDTH), BF), sds((TOK,...]
    all_gather x7 -> x0, blocking collectives: 150 us -> none  [the longest x1 24.3 us: per_device(): lax.all_gather(w_gate, 'dp', axis=0, tiled=True)]
    all_gather x4 -> x0, waiting for transfers between devices: 77.6 us -> none  [the longest x1 39.5 us: per_device(): lax.all_gather(grad_middle.astype(jnp.bfloat16), 'tensor', axis=0, tiled=...]
    dot_general x35 -> x0, matrix products: 74.8 us -> none  [the longest x7 19.5 us: cols_times(): lax.dot_general(left, right, (((0,), (0,)), ((), ())), preferred_element_...]
    psum x1 -> x0, blocking collectives: 67.5 us -> none  [per_device(): lax.psum((grad_gain_one, grad_gain_two, grad_gain_query, grad_gain_key),...]
    unnamed x1 -> x0, blocking collectives: 28.6 us -> none
    convert_element_type x19 -> x2, other arithmetic: 25.7 us -> 0.08 us  [the longest x1 0.07 us: per_device(): jnp.concatenate([attn_gain, mlp_gain]).astype(F32)[None]]
  transfers between devices with their start and end apart: 15 -> 0, of which waited for: 12 -> 0; matrix products, arithmetic and copies ran while one was open for 9% -> 0% of each run, Pallas kernels for 0% -> 0%
where the time goes in v1:
time: 287 us; the launch traced here: 284 us
  Pallas kernels  267 us (93%)
  local copies, waits for them, and re-layouts  10.3 us (4%)
  other arithmetic  5.5 us (2%)
    pallas_call x1, Pallas kernels, run_layer(): pl.pallas_call(layer_kernel, out_shape=(sds((TOK, WIDTH), BF), sds((TOK,...  267 us

profile of v1, /device:TPU:1, one launch (start us, length us, event | category | flops | bytes accessed | tf_op | source)
XLA Modules:
  0.0 284.1 jit_solution(276194786524253471)
XLA Ops:
  0.7 0.6 copy-done.12
  1.3 0.2 reduce-window.4
  1.5 0.1 convert_reduce_fusion
  1.6 0.1 select_reduce_fusion
  1.7 1.9 fusion
  3.6 1.3 pad_maximum_fusion
  4.9 0.0 copy-start.5
  4.9 1.1 copy.28.starts
  6.0 0.0 copy-done.11
  6.0 0.5 bitcast_convert_fusion
  6.5 0.0 copy-start.6
  6.5 0.0 copy-start.7
  6.6 0.0 copy-start.8
  6.6 0.0 copy-start.9
  6.6 0.7 pad_maximum_fusion.2.wm_own
  7.3 0.0 copy-done.6
  7.3 0.0 copy-done.7
  7.3 0.7 pad_maximum_fusion.3.wa_own
  8.0 0.0 copy-done.14
  8.0 0.1 maximum_convert_fusion
  8.1 0.6 broadcast_in_dim.38.gain_own
  8.7 267.5 %layer.1 = (bf16[128,1024]{1,0:T(8,128)(2,1)}, bf16[128,1024]{1,0:T(8,128)(2,1)}, f32[64,768]{1,0:T(8,128)}, f32[64,1152]{1,0:T(8,128)}, f32[24,128]{1,0:T(8,128)}) custom-call(bf16[64,768]{1,0:T(8,128)(2,1)} %pad_maximum_fusion.3.wa_own, bf16[64,1152]{1,0:T(8,128)(2,1)} %pad_maximum_fusion.2.wm_own, f32[8,128]{1,0:T(8,128)} %broadcast_in_dim.38.gain_own, ...), custom_call_target="tpu_custom_call" | custom-call | tf_op jit(solution)/shard_map/layer/pallas_call | solution.py:698
  276.2 0.7 slice_bitcast_fusion.2
  276.9 0.6 dynamic_slice.6
  277.4 0.6 dynamic_slice.7
  278.0 1.7 slice_bitcast_fusion
  279.8 0.7 slice_bitcast_fusion.1
  280.4 0.6 fusion.2
  281.1 1.3 slice_bitcast_fusion.4
  282.3 0.7 copy.31
  283.0 0.3 copy-done
  283.4 0.7 copy.32
  (22 shorter events, 0.1 us)
Async XLA Ops:
  0.6 0.7 copy-start.12
  4.9 1.1 copy-start.10
  4.9 1.1 copy-start.11
  4.9 1.6 copy-start.3
  4.9 1.6 copy-start.4
  4.9 1.6 copy-start.5
  6.5 0.8 copy-start.6
  6.5 0.8 copy-start.7
  6.6 0.8 copy-start.8
  6.6 0.7 copy-start.9
  7.3 0.7 copy-start.13
  7.3 0.7 copy-start.14
  278.0 1.7 copy-start.2
  279.8 2.6 copy-start.1
  282.3 1.0 copy-start

commit v2 on v1

v2 whole, which is shorter than its diff:
```python
import functools

import jax
import jax.numpy as jnp
from jax import lax
from jax.experimental import pallas as pl
from jax.experimental.pallas import tpu as pltpu
from jax.sharding import PartitionSpec as P

MESH = pl.DeviceIdType.MESH
BF = jnp.bfloat16
F32 = jnp.float32
HEAD = 128
EPS = 1e-06
ROPE_BASE = 1000000.0
MASKED = -1e30
SCALE = HEAD ** (-0.5)
TOK = 128
GROUP = 1024
WIDTH = 1024
NQ = 512
NO = 256
NM = 1152
CH = 256
N_SEMS = 240


def dot(a, b):
    return jnp.dot(a, b, preferred_element_type=F32)


def dot_nt(a, b):
    return lax.dot_general(a, b, (((1,), (1,)), ((), ())), preferred_element_type=F32)


def dot_tn(a, b):
    return lax.dot_general(a, b, (((0,), (0,)), ((), ())), preferred_element_type=F32)


class Links:
    def __init__(self, send_sems, recv_sems):
        self.send_sems, self.recv_sems = send_sems, recv_sems
        self.sends, self.recvs = 0, 0
        self.pending = []

    def recv_ids(self, count=1):
        first = self.recvs
        self.recvs += count
        assert self.recvs <= N_SEMS
        return first

    def copy(self, src, dst, device, send_id, recv_id):
        return pltpu.make_async_remote_copy(
            src_ref=src,
            dst_ref=dst,
            send_sem=self.send_sems.at[send_id],
            recv_sem=self.recv_sems.at[recv_id],
            device_id=device,
            device_id_type=MESH,
        )

    def send(self, src, dst, device, recv_id, when=None):
        copy = self.copy(src, dst, device, self.sends, recv_id)
        self.sends += 1
        assert self.sends <= N_SEMS
        if when is None:
            copy.start()
        else:
            pl.when(when)(copy.start)
        self.pending.append((copy, when))

    def wait(self, dst, device, recv_id, when=None):
        copy = self.copy(dst, dst, device, 0, recv_id)
        if when is None:
            copy.wait_recv()
        else:
            pl.when(when)(copy.wait_recv)

    def drain(self):
        for copy, when in self.pending:
            if when is None:
                copy.wait_send()
            else:
                pl.when(when)(copy.wait_send)


class Place:
    def __init__(self):
        d, t = lax.axis_index("dp"), lax.axis_index("tensor")
        self.d = d
        self.x, self.c = d // 4, d % 2
        self.y, self.z = (t // 4) * 2 + (d // 2) % 2, t % 4
        self.home = self.c == t // 4
        self.left_z, self.right_z = self.at(dz=3), self.at(dz=1)
        self.left_x, self.right_x = self.at(dx=3), self.at(dx=1)
        self.core = self.at(dc=1)
        self.swap = self.at(dy=2, dc=1)

    def device(self, x, y, z, c):
        return (x * 4 + (y % 2) * 2 + c, (y // 2) * 4 + z)

    def at(self, dx=0, dy=0, dz=0, dc=0):
        return self.device((self.x + dx) % 4, (self.y + dy) % 4, (self.z + dz) % 4, (self.c + dc) % 2)


class WeightGather:
    def __init__(self, links, place, own, buf):
        self.links, self.place, self.own, self.buf = links, place, own, buf
        self.y_id = links.recv_ids(4)
        self.ids = {name: links.recv_ids() for name in ("xm", "xp", "l", "r")}

    def block(self, index):
        return self.buf.at[pl.ds(pl.multiple_of(index * 64, 64), 64)]

    def rows(self, dx, half=None):
        first = ((self.place.x + dx) % 4) * 256
        if half is None:
            return self.buf.at[pl.ds(pl.multiple_of(first, 256), 256)]
        return self.buf.at[pl.ds(pl.multiple_of(first + 128 * half, 128), 128)]

    def begin(self):
        place, links = self.place, self.links
        side = place.y // 2
        for dy in (2, 1, 3, 0):
            device = place.device(place.x, (place.y + dy) % 4, place.z, side)
            links.send(
                self.own,
                self.block(place.d),
                device,
                self.y_id + place.d % 4,
                when=(place.c != side) if dy == 0 else None,
            )

        @pl.when(place.c == side)
        def _():
            self.block(place.d)[...] = self.own[...]

    def second(self):
        place, links = self.place, self.links
        for low in range(2):
            for core in range(2):
                y = 2 * place.c + low
                links.wait(
                    self.block(place.x * 4 + low * 2 + core),
                    place.device(place.x, y, place.z, core),
                    self.y_id + low * 2 + core,
                    when=(y != place.y) | (core != place.c),
                )
        mine = self.rows(0)
        links.send(mine, mine, place.right_x, self.ids["xm"])
        links.send(mine, mine, place.left_x, self.ids["xp"])

    def third(self):
        place, links = self.place, self.links
        links.wait(self.rows(3), place.left_x, self.ids["xm"])
        half = self.rows(3, 0)
        links.send(half, half, place.right_x, self.ids["l"])
        links.wait(self.rows(1), place.right_x, self.ids["xp"])
        half = self.rows(1, 1)
        links.send(half, half, place.left_x, self.ids["r"])

    def finish(self):
        place, links = self.place, self.links
        links.wait(self.rows(2, 0), place.left_x, self.ids["l"])
        links.wait(self.rows(2, 1), place.right_x, self.ids["r"])


class WeightSum:
    def __init__(self, links, place, full, side, land, out):
        self.links, self.place, self.full = links, place, full
        self.side, self.land, self.out = side, land, out
        self.ids = {n: links.recv_ids() for n in ("la", "lr", "ra", "rr", "lc", "rc")}
        self.y_id = links.recv_ids(4)

    def rows(self, dx, half):
        return pl.ds(pl.multiple_of(((self.place.x + dx) % 4) * 256 + 128 * half, 128), 128)

    def begin(self):
        place, links, side = self.place, self.links, self.side
        links.send(self.full.at[self.rows(2, 0)], side.at[0], place.right_x, self.ids["la"])
        links.send(self.full.at[self.rows(2, 1)], side.at[2], place.left_x, self.ids["ra"])
        links.send(self.full.at[self.rows(1, 1)], side.at[1], place.right_x, self.ids["lr"])
        links.send(self.full.at[self.rows(3, 0)], side.at[3], place.left_x, self.ids["rr"])

    def relay(self):
        place, links, side = self.place, self.links, self.side
        links.wait(side.at[0], place.left_x, self.ids["la"])
        side[6] = (self.full[self.rows(1, 0)].astype(F32) + side[0].astype(F32)).astype(BF)
        links.send(side.at[6], side.at[4], place.right_x, self.ids["lc"])
        links.wait(side.at[2], place.right_x, self.ids["ra"])
        side[7] = (self.full[self.rows(3, 1)].astype(F32) + side[2].astype(F32)).astype(BF)
        links.send(side.at[7], side.at[5], place.left_x, self.ids["rc"])

    def spread(self):
        place, links, side = self.place, self.links, self.side
        links.wait(side.at[1], place.left_x, self.ids["lr"])
        links.wait(side.at[3], place.right_x, self.ids["rr"])
        links.wait(side.at[4], place.left_x, self.ids["lc"])
        links.wait(side.at[5], place.right_x, self.ids["rc"])
        for half, first, other in ((0, 4, 3), (1, 5, 1)):
            side[8 + half] = (
                self.full[self.rows(0, half)].astype(F32)
                + side[first].astype(F32)
                + side[other].astype(F32)
            ).astype(BF)
        for low in range(2):
            for core in range(2):
                y = 2 * place.c + low
                away = (y != place.y) | (core != place.c)
                piece = side.at[8 + low, pl.ds(64 * core, 64)]
                links.send(
                    piece,
                    self.land.at[place.y],
                    place.device(place.x, y, place.z, core),
                    self.y_id + place.y,
                    when=away,
                )

                @pl.when(jnp.logical_not(away))
                def _():
                    self.land[place.y] = piece[...]

    def finish(self):
        place, links = self.place, self.links
        core = place.y // 2
        for k in range(4):
            y = (place.y + k) % 4
            links.wait(
                self.land.at[y],
                place.device(place.x, y, place.z, core),
                self.y_id + y,
                when=(place.c != core) if k == 0 else None,
            )
        total = self.land[0].astype(F32)
        for y in range(1, 4):
            total = total + self.land[y].astype(F32)
        self.out[...] = total


def token_rows(c, z, by_z):
    index = z * 2 + c if by_z else c * 4 + z
    return pl.multiple_of(index * TOK, TOK)


class TokenSum:
    def __init__(self, links, place, partial, core_in, side, by_z):
        self.links, self.place, self.partial = links, place, partial
        self.core_in, self.side, self.by_z = core_in, side, by_z
        self.core_id = links.recv_ids(4)
        self.ids = {n: links.recv_ids() for n in ("la", "lr", "ra", "rr", "lc", "rc")}

    def rows(self, c, z):
        return pl.ds(token_rows(c, z, self.by_z), TOK)

    def send_core(self, z, when=None):
        place = self.place
        self.links.send(
            self.partial.at[self.rows((place.c + 1) % 2, z)],
            self.core_in.at[z],
            place.core,
            self.core_id + z,
            when=when,
        )

    def half(self, z, h):
        return pl.ds(token_rows(self.place.c, z, self.by_z) + 64 * h, 64)

    def cross(self, k):
        place, links, side = self.place, self.links, self.side
        z = (place.z + k) % 4
        links.wait(self.core_in.at[z], place.core, self.core_id + z)
        rows = self.rows(place.c, z)
        self.partial[rows] = (
            self.partial[rows].astype(F32) + self.core_in[z].astype(F32)
        ).astype(BF)
        if k == 2:
            links.send(self.partial.at[self.half(z, 0)], side.at[0], place.right_z, self.ids["la"])
            links.send(self.partial.at[self.half(z, 1)], side.at[2], place.left_z, self.ids["ra"])
        if k == 1:
            links.send(self.partial.at[self.half(z, 1)], side.at[1], place.right_z, self.ids["lr"])
        if k == 3:
            links.send(self.partial.at[self.half(z, 0)], side.at[3], place.left_z, self.ids["rr"])

    def relay(self):
        place, links, side = self.place, self.links, self.side
        z = place.z
        links.wait(side.at[0], place.left_z, self.ids["la"])
        side[6] = (self.partial[self.half((z + 1) % 4, 0)].astype(F32) + side[0].astype(F32)).astype(BF)
        links.send(side.at[6], side.at[4], place.right_z, self.ids["lc"])
        links.wait(side.at[2], place.right_z, self.ids["ra"])
        side[7] = (self.partial[self.half((z + 3) % 4, 1)].astype(F32) + side[2].astype(F32)).astype(BF)
        links.send(side.at[7], side.at[5], place.left_z, self.ids["rc"])

    def total(self):
        place, links, side = self.place, self.links, self.side
        links.wait(side.at[1], place.left_z, self.ids["lr"])
        links.wait(side.at[3], place.right_z, self.ids["rr"])
        links.wait(side.at[4], place.left_z, self.ids["lc"])
        links.wait(side.at[5], place.right_z, self.ids["rc"])
        parts = []
        for half, first, other in ((0, 4, 3), (1, 5, 1)):
            parts.append(
                self.partial[self.half(place.z, half)].astype(F32)
                + side[first].astype(F32)
                + side[other].astype(F32)
            )
        return jnp.concatenate(parts, axis=0)


class TokenGather:
    def __init__(self, links, place, buf, by_z):
        self.links, self.place, self.buf, self.by_z = links, place, buf, by_z
        names = ("zm", "zp", "l", "r", "c0", "c1", "c2", "c3")
        self.ids = {name: links.recv_ids() for name in names}

    def rows(self, k, core=0, half=None):
        place = self.place
        first = token_rows((place.c + core) % 2, (place.z + k) % 4, self.by_z)
        if half is None:
            return self.buf.at[pl.ds(first, TOK)]
        return self.buf.at[pl.ds(first + 64 * half, 64)]

    def push(self, ref, device, name):
        self.links.send(ref, ref, device, self.ids[name])

    def begin(self):
        place, own = self.place, self.rows(0)
        self.push(own, place.right_z, "zm")
        self.push(own, place.left_z, "zp")
        self.push(own, place.core, "c0")

    def sides(self):
        place = self.place
        self.links.wait(self.rows(3), place.left_z, self.ids["zm"])
        self.push(self.rows(3, half=0), place.right_z, "l")
        self.push(self.rows(3), place.core, "c3")
        self.links.wait(self.rows(1), place.right_z, self.ids["zp"])
        self.push(self.rows(1, half=1), place.left_z, "r")
        self.push(self.rows(1), place.core, "c1")

    def far(self):
        place = self.place
        self.links.wait(self.rows(2, half=0), place.left_z, self.ids["l"])
        self.links.wait(self.rows(2, half=1), place.right_z, self.ids["r"])
        self.push(self.rows(2), place.core, "c2")

    def core(self, k):
        self.links.wait(self.rows(k, core=1), self.place.core, self.ids["c%d" % k])


def layer_kernel(
    wq_own,
    wo_own,
    wm_own,
    gain_own,
    x_own,
    og_own,
    query_gain,
    key_gain,
    trig_own,
    starts_own,
    out_ref,
    in_grad_ref,
    gq_ref,
    go_ref,
    gm_ref,
    gains_ref,
    wq,
    wo,
    wm,
    gain_in,
    gain_one,
    gain_two,
    trig,
    starts,
    cosine,
    sine,
    xs,
    ogs,
    h1,
    r1,
    qk_pre,
    q_rot,
    k_rot,
    vals,
    mixed,
    lse,
    p1,
    p1_core,
    p1_side,
    middle,
    h2,
    grad_act,
    act,
    dgu,
    p2,
    p2_core,
    p2_side,
    po,
    po_core,
    po_side,
    gb,
    grad_mid,
    dk,
    dv,
    dqkv,
    p3,
    p3_core,
    p3_side,
    gm_full,
    gm_side,
    gm_land,
    gq_full,
    gq_side,
    gq_land,
    go_full,
    go_side,
    go_land,
    out_tmp,
    in_grad_tmp,
    gg,
    gg_y,
    gg_a,
    gg_x,
    gg_b,
    gg_z,
    send_sems,
    recv_sems,
):
    links = Links(send_sems, recv_sems)
    place = Place()
    x, y, z, c = place.x, place.y, place.z, place.c
    home, away = place.home, jnp.logical_not(place.home)
    own = pl.ds(token_rows(c, z, False), TOK)
    own_z = pl.ds(token_rows(c, z, True), TOK)
    swap_own = pl.ds(token_rows((c + 1) % 2, z, False), TOK)
    swap_z = pl.ds(token_rows((c + 1) % 2, z, True), TOK)
    column = [(dy, dc) for dy in range(4) for dc in range(2) if dy or dc]

    barrier = pltpu.get_barrier_semaphore()
    for peer in (
        [place.at(dy=dy, dc=dc) for dy, dc in column]
        + [place.at(dx=k) for k in range(1, 4)]
        + [place.at(dz=k) for k in range(1, 4)]
    ):
        pl.semaphore_signal(barrier, inc=1, device_id=peer, device_id_type=MESH)

    gather_q = WeightGather(links, place, wq_own, wq)
    gather_o = WeightGather(links, place, wo_own, wo)
    gather_m = WeightGather(links, place, wm_own, wm)
    gather_x = TokenGather(links, place, xs, False)
    gather_og = TokenGather(links, place, ogs, True)
    gather_h2 = TokenGather(links, place, h2, True)
    gather_gb = TokenGather(links, place, gb, False)
    sum_1 = TokenSum(links, place, p1, p1_core, p1_side, False)
    sum_2 = TokenSum(links, place, p2, p2_core, p2_side, True)
    sum_o = TokenSum(links, place, po, po_core, po_side, True)
    sum_3 = TokenSum(links, place, p3, p3_core, p3_side, False)
    weight_m = WeightSum(links, place, gm_full, gm_side, gm_land, gm_ref)
    weight_q = WeightSum(links, place, gq_full, gq_side, gq_land, gq_ref)
    weight_o = WeightSum(links, place, go_full, go_side, go_land, go_ref)
    x_id, og_id, trig_id, starts_id, out_id, in_grad_id = [links.recv_ids() for _ in range(6)]
    gain_id, gain_x_id = links.recv_ids(4), links.recv_ids(4)
    gg_y_id, gg_x_id, gg_z_id = links.recv_ids(8), links.recv_ids(4), links.recv_ids(4)

    @pl.when(home)
    def _():
        xs[own] = x_own[...]
        ogs[own_z] = og_own[...]
        trig[...] = trig_own[...]
        starts[...] = starts_own[...]

    gain_in[place.d] = gain_own[...]

    pl.semaphore_wait(barrier, 13)

    links.send(x_own, xs.at[swap_own], place.swap, x_id, when=away)
    gather_q.begin()
    for dy, dc in ((0, 1), (1, 0), (1, 1)):
        other_y = (y // 2) * 2 + (y % 2 + dy) % 2
        peer = place.device(x, other_y, z, (c + dc) % 2)
        links.send(gain_in.at[place.d], gain_in.at[place.d], peer, gain_id + place.d % 4)
    links.send(trig_own, trig, place.core, trig_id, when=home)
    links.send(starts_own, starts, place.core, starts_id, when=home)
    gather_o.begin()

    links.wait(xs.at[own], place.swap, x_id, when=away)
    gather_x.begin()
    gather_q.second()
    for dy, dc in ((0, 1), (1, 0), (1, 1)):
        other_y = (y // 2) * 2 + (y % 2 + dy) % 2
        index = x * 4 + (other_y % 2) * 2 + (c + dc) % 2
        peer = place.device(x, other_y, z, (c + dc) % 2)
        links.wait(gain_in.at[index], peer, gain_id + index % 4)
    four = pl.ds(x * 4, 4)
    for k in range(1, 4):
        links.send(gain_in.at[four], gain_in.at[four], place.at(dx=k), gain_x_id + x)
    gather_o.second()
    links.send(og_own, ogs.at[swap_z], place.swap, og_id, when=away)

    gather_x.sides()
    gather_q.third()
    gather_m.begin()
    for k in range(1, 4):
        other = (x + k) % 4
        links.wait(gain_in.at[pl.ds(other * 4, 4)], place.at(dx=k), gain_x_id + other)
    low = lax.broadcasted_iota(jnp.int32, (1, 128), 1) < 64
    for k in range(8):
        even, odd = gain_in[2 * k][0:1], gain_in[2 * k + 1][0:1]
        cols = slice(128 * k, 128 * k + 128)
        gain_one[0:1, cols] = jnp.where(low, even, pltpu.roll(odd, 64, 1))
        gain_two[0:1, cols] = jnp.where(low, pltpu.roll(even, 64, 1), odd)

    links.wait(trig, place.core, trig_id, when=away)
    links.wait(starts, place.core, starts_id, when=away)

    def trig_chunk(i, carry):
        rows = pl.ds(pl.multiple_of(i * CH, CH), CH)
        pair = trig[rows]
        turned = pltpu.roll(pair, 64, 1)
        cosine[rows] = jnp.where(low, pair, turned)
        sine[rows] = jnp.where(low, -turned, pair)
        return carry

    lax.fori_loop(0, 4, trig_chunk, 0)

    gather_x.far()
    gather_o.third()
    for k in range(4):
        gather_x.core(k)
    links.wait(ogs.at[own_z], place.swap, og_id, when=away)
    gather_og.begin()

    def norm_chunk(i, carry):
        rows = pl.ds(pl.multiple_of(i * 128, 128), 128)
        wide = xs[rows].astype(F32)
        r = lax.rsqrt(jnp.mean(wide * wide, axis=-1, keepdims=True) + EPS)
        r1[rows] = r
        h1[rows] = (wide * r * gain_one[0:1]).astype(BF)
        return carry

    lax.fori_loop(0, 8, norm_chunk, 0)
    gather_q.finish()
    gather_m.second()

    def qkv_chunk(i, carry):
        rows = pl.ds(pl.multiple_of(i * CH, CH), CH)
        pre = dot(h1[rows], wq[...])
        qk_pre[rows] = pre[:, 0:384]
        vals[rows] = pre[:, 384:512].astype(BF)
        cos, sin = cosine[rows], sine[rows]
        for h in range(3):
            part = pre[:, 128 * h : 128 * h + 128]
            r = lax.rsqrt(jnp.mean(part * part, axis=-1, keepdims=True) + EPS)
            scaled = part * r * (query_gain if h < 2 else key_gain)[0:1]
            turned = (scaled * cos + pltpu.roll(scaled, 64, 1) * sin).astype(BF)
            if h < 2:
                q_rot[h, rows] = turned
            else:
                k_rot[rows] = turned
        return carry

    lax.fori_loop(0, 4, qkv_chunk, 0)
    gather_o.finish()
    gather_og.sides()

    def allowed(qb, keys):
        key_at = lax.broadcasted_iota(jnp.int32, (CH, keys), 1)
        query_at = lax.broadcasted_iota(jnp.int32, (CH, keys), 0) + qb * CH
        return (key_at >= starts[qb * CH : qb * CH + CH]) & (key_at <= query_at)

    def send_chunk(group_sum, qb):
        for b in (2 * qb, 2 * qb + 1):
            group_sum.send_core(b % 4, when=c != b // 4)

    for qb in range(4):
        rows = slice(qb * CH, qb * CH + CH)
        keys = CH * (qb + 1)
        ok = allowed(qb, keys)
        for h in range(2):
            scores = jnp.where(ok, dot_nt(q_rot[h, rows], k_rot[0:keys]) * SCALE, MASKED)
            top = jnp.max(scores, axis=-1, keepdims=True)
            terms = jnp.exp(scores - top)
            total = jnp.sum(terms, axis=-1, keepdims=True)
            lse[h, rows] = top + jnp.log(total)
            weights = (terms * (1.0 / total)).astype(BF)
            mixed[rows, 128 * h : 128 * h + 128] = dot(weights, vals[0:keys]).astype(BF)
        p1[rows] = dot_nt(mixed[rows], wo[...]).astype(BF)
        send_chunk(sum_1, qb)
        if qb == 1:
            gather_m.third()

    for k in (2, 1, 3, 0):
        sum_1.cross(k)
    gather_og.far()
    sum_1.relay()
    gather_m.finish()
    for k in range(4):
        gather_og.core(k)

    def grad_act_chunk(i, carry):
        rows = pl.ds(pl.multiple_of(i * CH, CH), CH)
        grad_act[rows] = dot(ogs[rows], wm[:, 768:1152])
        return carry

    lax.fori_loop(0, 4, grad_act_chunk, 0)

    mid = xs[own].astype(F32) + sum_1.total()
    middle[...] = mid
    r_two = lax.rsqrt(jnp.mean(mid * mid, axis=-1, keepdims=True) + EPS)
    h2[own_z] = (mid * r_two * gain_two[0:1]).astype(BF)
    gather_h2.begin()

    def mlp_chunk(k):
        gather_h2.core(k)
        at = (z + k) % 4
        rows = pl.ds(pl.multiple_of(at * CH, CH), CH)
        pre = dot(h2[rows], wm[:, 0:768])
        gate, up = pre[:, 0:384], pre[:, 384:768]
        sig = 1.0 / (1.0 + jnp.exp(-gate))
        silu = gate * sig
        acted = (silu * up).astype(BF)
        act[rows] = acted
        grad = grad_act[rows]
        dgu[rows, 0:384] = (grad * up * (sig * (1.0 + gate * (1.0 - sig)))).astype(BF)
        dgu[rows, 384:768] = (grad * silu).astype(BF)
        p2[rows] = dot_nt(dgu[rows], wm[:, 0:768]).astype(BF)
        sum_2.send_core(at)

    def down_chunk(i, carry):
        rows = pl.ds(pl.multiple_of(i * CH, CH), CH)
        po[rows] = dot_nt(act[rows], wm[:, 768:1152]).astype(BF)
        return carry

    mlp_chunk(0)
    gather_h2.sides()
    mlp_chunk(3)
    mlp_chunk(1)
    sum_2.cross(3)
    sum_2.cross(1)
    gather_h2.far()
    mlp_chunk(2)
    sum_2.cross(2)
    sum_2.cross(0)

    lax.fori_loop(0, 4, down_chunk, 0)
    sum_2.relay()
    for k in range(4):
        sum_o.send_core(k)

    def mlp_weight_chunk(i, carry):
        cols = pl.ds(pl.multiple_of(i * CH, CH), CH)
        gm_full[cols, 0:768] = dot_tn(h2[:, cols], dgu[...]).astype(BF)
        gm_full[cols, 768:1152] = dot_tn(ogs[:, cols], act[...]).astype(BF)
        return carry

    lax.fori_loop(0, 4, mlp_weight_chunk, 0)
    weight_m.begin()

    err = sum_2.total()
    mid = middle[...]
    r_two = lax.rsqrt(jnp.mean(mid * mid, axis=-1, keepdims=True) + EPS)
    normed = mid * r_two
    part = jnp.sum(err * normed, axis=0, keepdims=True)
    gg[...] = jnp.zeros_like(gg)
    for k in range(8):
        gg[8 + k : 9 + k] = part[:, 128 * k : 128 * k + 128]
    scaled = err * gain_two[0:1]
    grad = ogs[own_z].astype(F32) + r_two * (
        scaled - normed * jnp.mean(scaled * normed, axis=-1, keepdims=True)
    )
    grad_mid[...] = grad
    gb[own] = grad.astype(BF)
    gather_gb.begin()
    dk[...] = jnp.zeros_like(dk)
    dv[...] = jnp.zeros_like(dv)
    gather_gb.sides()
    for k in (2, 1, 3, 0):
        sum_o.cross(k)
    weight_m.relay()
    gather_gb.far()
    for k in range(4):
        gather_gb.core(k)

    def out_weight_chunk(i, carry):
        cols = pl.ds(pl.multiple_of(i * CH, CH), CH)
        go_full[cols] = dot_tn(gb[:, cols], mixed[...]).astype(BF)
        return carry

    def back_rope(turned, pre, gain, cos, sin):
        r = lax.rsqrt(jnp.mean(pre * pre, axis=-1, keepdims=True) + EPS)
        normed = pre * r
        err = turned * cos - pltpu.roll(turned, 64, 1) * sin
        scaled = err * gain
        grad = r * (scaled - normed * jnp.mean(scaled * normed, axis=-1, keepdims=True))
        return grad, jnp.sum(err * normed, axis=0, keepdims=True)

    attn_part = jnp.zeros((1, WIDTH), F32)
    for qb in (3, 2, 1, 0):
        rows = slice(qb * CH, qb * CH + CH)
        keys = CH * (qb + 1)
        ok = allowed(qb, keys)
        cos, sin = cosine[rows], sine[rows]
        grad_mixed = dot(gb[rows], wo[...]).astype(BF)
        for h in range(2):
            grad_h = grad_mixed[:, 128 * h : 128 * h + 128]
            scores = jnp.where(ok, dot_nt(q_rot[h, rows], k_rot[0:keys]) * SCALE, MASKED)
            probs = jnp.exp(scores - lse[h, rows])
            grad_probs = dot_nt(grad_h, vals[0:keys])
            inner = jnp.sum(probs * grad_probs, axis=-1, keepdims=True)
            grad_scores = (probs * (grad_probs - inner)).astype(BF)
            dk[0:keys] += dot_tn(grad_scores, q_rot[h, rows]) * SCALE
            dv[0:keys] += dot_tn(probs.astype(BF), grad_h)
            grad_q = (dot(grad_scores, k_rot[0:keys]) * SCALE).astype(BF).astype(F32)
            pre = qk_pre[rows, 128 * h : 128 * h + 128]
            grad, gain_part = back_rope(grad_q, pre, query_gain[0:1], cos, sin)
            dqkv[rows, 128 * h : 128 * h + 128] = grad.astype(BF)
            gg[16:17] += gain_part
        grad_k = dk[rows].astype(BF).astype(F32)
        grad, gain_part = back_rope(grad_k, qk_pre[rows, 256:384], key_gain[0:1], cos, sin)
        dqkv[rows, 256:384] = grad.astype(BF)
        gg[17:18] += gain_part
        dqkv[rows, 384:512] = dv[rows].astype(BF)
        err = dot_nt(dqkv[rows], wq[...])
        p3[rows] = err.astype(BF)
        send_chunk(sum_3, qb)
        attn_part += jnp.sum(err * (xs[rows].astype(F32) * r1[rows]), axis=0, keepdims=True)
        if qb == 3:
            sum_o.relay()
        if qb == 2:
            weight_m.spread()

    for k in (2, 1, 3, 0):
        sum_3.cross(k)
    for k in range(8):
        gg[k : k + 1] = attn_part[:, 128 * k : 128 * k + 128]
    for dy, dc in column:
        links.send(gg, gg_y.at[y * 2 + c], place.at(dy=dy, dc=dc), gg_y_id + y * 2 + c)

    def attn_weight_chunk(i, carry):
        cols = pl.ds(pl.multiple_of(i * CH, CH), CH)
        gq_full[cols] = dot_tn(h1[:, cols], dqkv[...]).astype(BF)
        return carry

    lax.fori_loop(0, 4, attn_weight_chunk, 0)
    weight_q.begin()
    sum_3.relay()
    lax.fori_loop(0, 4, out_weight_chunk, 0)
    weight_o.begin()

    out_tmp[...] = (middle[...] + sum_o.total()).astype(BF)
    links.send(out_tmp, out_ref, place.swap, out_id, when=away)

    gg_y[y * 2 + c] = gg[...]
    for dy, dc in column:
        index = ((y + dy) % 4) * 2 + (c + dc) % 2
        links.wait(gg_y.at[index], place.at(dy=dy, dc=dc), gg_y_id + index)
    total = gg_y[0]
    for k in range(1, 8):
        total = total + gg_y[k]
    gg_a[...] = total
    for k in range(1, 4):
        links.send(gg_a, gg_x.at[x], place.at(dx=k), gg_x_id + x)
    weight_q.relay()
    weight_o.relay()

    err = sum_3.total()
    r_one = r1[own]
    normed = xs[own].astype(F32) * r_one
    scaled = err * gain_one[0:1]
    in_grad_tmp[...] = (
        grad_mid[...]
        + r_one * (scaled - normed * jnp.mean(scaled * normed, axis=-1, keepdims=True))
    ).astype(BF)
    links.send(in_grad_tmp, in_grad_ref, place.swap, in_grad_id, when=away)

    gg_x[x] = gg_a[...]
    for k in range(1, 4):
        other = (x + k) % 4
        links.wait(gg_x.at[other], place.at(dx=k), gg_x_id + other)
    gg_b[...] = (gg_x[0] + gg_x[1]) + (gg_x[2] + gg_x[3])
    for k in range(1, 4):
        links.send(gg_b, gg_z.at[z], place.at(dz=k), gg_z_id + z)

    weight_q.spread()
    weight_o.spread()
    weight_m.finish()

    @pl.when(home)
    def _():
        out_ref[...] = out_tmp[...]
        in_grad_ref[...] = in_grad_tmp[...]

    gg_z[z] = gg_b[...]
    for k in range(1, 4):
        other = (z + k) % 4
        links.wait(gg_z.at[other], place.at(dz=k), gg_z_id + other)
    gains_ref[...] = (gg_z[0] + gg_z[1]) + (gg_z[2] + gg_z[3])

    weight_q.finish()
    weight_o.finish()
    links.wait(out_ref, place.swap, out_id, when=away)
    links.wait(in_grad_ref, place.swap, in_grad_id, when=away)
    links.drain()


def run_layer(*args):
    vmem = pl.BlockSpec(memory_space=pltpu.VMEM)

    def sds(shape, kind):
        return jax.ShapeDtypeStruct(shape, kind)

    def buf(shape, kind=BF):
        return pltpu.VMEM(shape, kind)

    group = (GROUP, WIDTH)
    table = (GROUP, HEAD)
    block = (TOK, WIDTH)
    landing = [buf(group), buf((4, TOK, WIDTH)), buf((8, 64, WIDTH))]
    gains = (24, 128)

    def weight_landing(cols):
        return [buf((WIDTH, cols)), buf((10, 128, cols)), buf((4, 64, cols))]

    scratch = [
        buf((WIDTH, NQ)),
        buf((WIDTH, NO)),
        buf((WIDTH, NM)),
        buf((16, 8, 128), F32),
        buf((1, WIDTH), F32),
        buf((1, WIDTH), F32),
        buf(table, F32),
        buf((GROUP, 1), jnp.int32),
        buf(table, F32),
        buf(table, F32),
        buf(group),
        buf(group),
        buf(group),
        buf((GROUP, 1), F32),
        buf((GROUP, 384), F32),
        buf((2, GROUP, HEAD)),
        buf(table),
        buf(table),
        buf((GROUP, 256)),
        buf((2, GROUP, 1), F32),
        *landing,
        buf(block, F32),
        buf(group),
        buf((GROUP, 384), F32),
        buf((GROUP, 384)),
        buf((GROUP, 768)),
        *landing,
        *landing,
        buf(group),
        buf(block, F32),
        buf(table, F32),
        buf(table, F32),
        buf((GROUP, 512)),
        *landing,
        *weight_landing(NM),
        *weight_landing(NQ),
        *weight_landing(NO),
        buf(block),
        buf(block),
        buf(gains, F32),
        buf((8, *gains), F32),
        buf(gains, F32),
        buf((4, *gains), F32),
        buf(gains, F32),
        buf((4, *gains), F32),
        pltpu.SemaphoreType.DMA((N_SEMS,)),
        pltpu.SemaphoreType.DMA((N_SEMS,)),
    ]
    return pl.pallas_call(
        layer_kernel,
        out_shape=(
            sds(block, BF),
            sds(block, BF),
            sds((64, NQ), F32),
            sds((64, NO), F32),
            sds((64, NM), F32),
            sds(gains, F32),
        ),
        in_specs=[vmem] * len(args),
        out_specs=(vmem,) * 6,
        scratch_shapes=scratch,
        name="layer",
        compiler_params=pltpu.CompilerParams(
            collective_id=0, has_side_effects=True, vmem_limit_bytes=63 * 2**20
        ),
    )(*args)


def tables(lengths):
    ends = jnp.cumsum(lengths)
    begins = ends - lengths
    at = jnp.arange(GROUP, dtype=jnp.int32)
    label = jnp.sum((at[:, None] >= ends[None, :]).astype(jnp.int32), axis=1)
    chosen = label[:, None] == jnp.arange(lengths.shape[0], dtype=jnp.int32)[None, :]
    starts = jnp.sum(jnp.where(chosen, begins[None, :], 0), axis=1)
    half = HEAD // 2
    frequency = ROPE_BASE ** (-(jnp.arange(half).astype(F32) * 2.0 / HEAD))
    angles = (at - starts).astype(F32)[:, None] * frequency[None, :]
    cos, sin = jnp.cos(angles), jnp.sin(angles)
    return jnp.concatenate([cos, sin], axis=-1), starts[:, None]


def per_device(
    layer_input,
    seq_lengths,
    attn_gain,
    w_query,
    key_projection,
    value_projection,
    query_gain,
    key_gain,
    w_out,
    mlp_gain,
    w_gate,
    w_up,
    w_down,
    out_grad,
):
    trig, starts = tables(seq_lengths[0])
    wq_own = jnp.concatenate([w_query, key_projection, value_projection], axis=1)
    wm_own = jnp.concatenate([w_gate, w_up, w_down.T], axis=1)
    gain_own = jnp.broadcast_to(jnp.concatenate([attn_gain, mlp_gain]).astype(F32)[None], (8, 128))
    out, in_grad, gq, go, gm, gains = run_layer(
        wq_own,
        w_out.T,
        wm_own,
        gain_own,
        layer_input,
        out_grad,
        query_gain.astype(F32)[None],
        key_gain.astype(F32)[None],
        trig,
        starts,
    )
    piece = attn_gain.shape[0]
    first = lax.axis_index("dp") * piece
    grad_attn_gain = lax.dynamic_slice_in_dim(gains[0:8].reshape(-1), first, piece, 0)
    grad_mlp_gain = lax.dynamic_slice_in_dim(gains[8:16].reshape(-1), first, piece, 0)
    return (
        out,
        in_grad,
        grad_attn_gain,
        gq[:, 0:256],
        gq[:, 256:384],
        gq[:, 384:512],
        gains[16],
        gains[17],
        go.T,
        grad_mlp_gain,
        gm[:, 0:384],
        gm[:, 384:768],
        gm[:, 768:1152].T,
    )


def solution(mesh):
    both = P(("dp", "tensor"), None)
    split = P("dp", "tensor")
    turned = P("tensor", "dp")
    in_specs = (
        both,
        P("dp", None),
        P("dp"),
        split,
        split,
        split,
        P(),
        P(),
        turned,
        P("dp"),
        split,
        split,
        turned,
        both,
    )
    out_specs = (both, both, P("dp"), split, split, split, P(), P(), turned, P("dp"), split, split, turned)
    return jax.shard_map(
        per_device, mesh=mesh, in_specs=in_specs, out_specs=out_specs, check_vma=False
    )
```

time: 287 us -> 164 us (0.57)
  Pallas kernels: 267 us -> 146 us
    pallas_call x1, Pallas kernels: 267 us -> 146 us  [run_layer(): pl.pallas_call(layer_kernel, out_shape=(sds(block, BF), sds(block, BF), s...]
where the time goes in v2:
time: 164 us; the launch traced here: 163 us
  Pallas kernels  146 us (89%)
  local copies, waits for them, and re-layouts  11 us (7%)
  other arithmetic  5.15 us (3%)
    pallas_call x1, Pallas kernels, run_layer(): pl.pallas_call(layer_kernel, out_shape=(sds(block, BF), sds(block, BF), s...  146 us
    unnamed x33, local copies, waits for them, and re-layouts  3.3 us

profile of v2, /device:TPU:1, one launch (start us, length us, event | category | flops | bytes accessed | tf_op | source)
XLA Modules:
  0.0 163.2 jit_solution(18176945470160499700)
XLA Ops:
  0.7 0.6 copy-done.12
  1.3 0.2 reduce-window.4
  1.5 0.1 convert_reduce_fusion
  1.6 0.1 select_reduce_fusion
  1.7 1.9 %multiply_cosine_fusion = (f32[1024,64]{1,0:T(8,128)S(1)}, f32[1024,64]{1,0:T(8,128)S(1)}) fusion(f32[64]{0:T(128)S(1)} %negate_power_fusion, f32[1024]{0:T(1024)S(1)} %subtract_convert_fusion), kind=kLoop, calls=%fused_computation.1 | loop fusion | flops 65536 | bytes 528640 | tf_op jit(solution)/shard_map/cos | solution.py:904
  3.6 1.0 pad_maximum_fusion.trig_own
  4.6 0.0 copy-start.6
  4.6 1.0 copy.28.starts_own
  5.6 0.5 bitcast_convert_fusion
  6.2 0.0 copy-start.7
  6.2 0.0 copy-start.8
  6.2 0.0 copy-start.9
  6.2 0.7 pad_maximum_fusion.1.wm_own
  6.9 0.0 copy-done.7
  6.9 0.6 pad_maximum_fusion.2.wq_own
  7.6 0.0 copy-done.13
  7.6 0.0 copy-done.14
  7.6 0.1 maximum_convert_fusion
  7.7 0.6 broadcast_in_dim.38.gain_own
  8.3 146.2 %layer.1 = (bf16[128,1024]{1,0:T(8,128)(2,1)}, bf16[128,1024]{1,0:T(8,128)(2,1)}, f32[64,512]{1,0:T(8,128)}, f32[64,256]{1,0:T(8,128)}, f32[64,1152]{1,0:T(8,128)}, /*index=5*/f32[24,128]{1,0:T(8,128)}) custom-call(bf16[64,512]{1,0:T(8,128)(2,1)} %pad_maximum_fusion.2.wq_own, bf16[64,256]{1,0:T(8,128)(2,1)} %bitcast.31, ...), custom_call_target="tpu_custom_call" | custom-call | tf_op jit(solution)/shard_map/layer/pallas_call | solution.py:874
  154.5 0.7 slice_bitcast_fusion.1
  155.2 0.6 dynamic_slice.6
  155.8 0.6 dynamic_slice.7
  156.4 1.7 %slice_bitcast_fusion = (f32[384,64]{0,1:T(8,128)}, f32[64,384]{1,0:T(8,128)}, f32[64,384]{1,0:T(8,128)}) fusion(f32[64,1152]{1,0:T(8,128)} %get-tuple-element.24), kind=kLoop, calls=%fused_computation.4 | loop fusion | bytes 589824 | tf_op jit(solution)/shard_map/transpose | solution.py:957
  158.1 0.6 fusion.1
  158.7 1.3 slice_bitcast_fusion.3
  160.0 0.6 slice.31
  160.7 0.7 copy.32
  161.4 0.3 copy-done
  161.7 0.7 copy.33
  162.4 0.2 copy-done.3
  162.6 0.6 copy.34
  (23 shorter events, 0.1 us)
Async XLA Ops:
  0.6 0.7 copy-start.12
  4.6 1.0 copy-start.10
  4.6 1.0 copy-start.11
  4.6 1.6 copy-start.4
  4.6 1.6 copy-start.5
  4.6 1.6 copy-start.6
  6.2 0.8 copy-start.7
  6.2 0.8 copy-start.8
  6.2 0.7 copy-start.9
  6.9 0.7 copy-start.13
  6.9 0.7 copy-start.14
  156.4 1.7 %copy-start.2 = (f32[64,512]{1,0:T(8,128)S(1)}, f32[64,512]{1,0:T(8,128)}, u32[]{:S(2)}) copy-start(f32[64,512]{1,0:T(8,128)} %get-tuple-element.22) | copy-start | bytes 393220
  158.1 2.5 %copy-start.1 = (bf16[128,1024]{1,0:T(8,128)(2,1)S(1)}, bf16[128,1024]{1,0:T(8,128)(2,1)}, u32[]{:S(2)}) copy-start(bf16[128,1024]{1,0:T(8,128)(2,1)} %get-tuple-element.51) | copy-start | bytes 786436
  160.7 1.0 copy-start
  161.7 0.9 copy-start.3

commit v3 on v2

--- a/solution.py
+++ b/solution.py
@@ -20,7 +20,8 @@
 WIDTH = 1024
 NQ = 512
 NO = 256
-NM = 1152
+NU = 768
+ND = 384
 CH = 256
 N_SEMS = 240
 
@@ -191,7 +192,7 @@
         side[7] = (self.full[self.rows(3, 1)].astype(F32) + side[2].astype(F32)).astype(BF)
         links.send(side.at[7], side.at[5], place.left_x, self.ids["rc"])
 
-    def spread(self):
+    def gathered(self):
         place, links, side = self.place, self.links, self.side
         links.wait(side.at[1], place.left_x, self.ids["lr"])
         links.wait(side.at[3], place.right_x, self.ids["rr"])
@@ -203,6 +204,10 @@
                 + side[first].astype(F32)
                 + side[other].astype(F32)
             ).astype(BF)
+
+    def spread(self):
+        self.gathered()
+        place, links, side = self.place, self.links, self.side
         for low in range(2):
             for core in range(2):
                 y = 2 * place.c + low
@@ -237,6 +242,208 @@
         self.out[...] = total
 
 
+class WeightSumDirect(WeightSum):
+    def begin(self):
+        place = self.place
+        for k, name in ((2, "ra"), (1, "la"), (3, "lr")):
+            self.links.send(
+                self.full.at[pl.ds(((place.x + k) % 4) * 2, 2)],
+                self.side.at[pl.ds(2 * (k - 1), 2)],
+                place.at(dx=k),
+                self.ids[name],
+            )
+
+    def gathered(self):
+        place, side = self.place, self.side
+        for k, name in ((1, "la"), (3, "lr"), (2, "ra")):
+            self.links.wait(side.at[pl.ds(2 * (k - 1), 2)], place.at(dx=4 - k), self.ids[name])
+        for half in range(2):
+            total = self.full[place.x * 2 + half].astype(F32)
+            for k in range(3):
+                total = total + side[2 * k + half].astype(F32)
+            side[8 + half] = total.astype(BF)
+
+
+class WeightGatherX:
+    def __init__(self, links, place, own, stage, buf):
+        self.links, self.place, self.own, self.stage, self.buf = links, place, own, stage, buf
+        self.y_id = links.recv_ids(4)
+        self.ids = {name: links.recv_ids() for name in ("xm", "xp", "l", "r")}
+
+    def block(self, dx, half=None):
+        at = (self.place.x + dx) % 4
+        if half is None:
+            return self.stage.at[at]
+        return self.stage.at[at, pl.ds(32 * half, 32)]
+
+    def begin(self):
+        place, links = self.place, self.links
+        links.send(self.own, self.block(0), place.right_x, self.ids["xm"])
+        links.send(self.own, self.block(0), place.left_x, self.ids["xp"])
+        self.stage[place.x] = self.own[...]
+
+    def relay(self):
+        place, links = self.place, self.links
+        links.wait(self.block(3), place.left_x, self.ids["xm"])
+        links.send(self.block(3, 0), self.block(3, 0), place.right_x, self.ids["l"])
+        links.wait(self.block(1), place.right_x, self.ids["xp"])
+        links.send(self.block(1, 1), self.block(1, 1), place.left_x, self.ids["r"])
+
+    def spread(self):
+        place, links = self.place, self.links
+        links.wait(self.block(2, 0), place.left_x, self.ids["l"])
+        links.wait(self.block(2, 1), place.right_x, self.ids["r"])
+        side = place.y // 2
+        for dy in (2, 1, 3, 0):
+            links.send(
+                self.stage,
+                self.buf.at[:, place.d % 4],
+                place.device(place.x, (place.y + dy) % 4, place.z, side),
+                self.y_id + place.d % 4,
+                when=(place.c != side) if dy == 0 else None,
+            )
+
+        @pl.when(place.c == side)
+        def _():
+            self.buf[:, place.d % 4] = self.stage[...]
+
+    def finish(self):
+        place, links = self.place, self.links
+        for low in range(2):
+            for core in range(2):
+                y = 2 * place.c + low
+                links.wait(
+                    self.buf.at[:, low * 2 + core],
+                    place.device(place.x, y, place.z, core),
+                    self.y_id + low * 2 + core,
+                    when=(y != place.y) | (core != place.c),
+                )
+
+
+class WeightSumY:
+    def __init__(self, links, place, full, land, total, side, last, out):
+        self.links, self.place, self.full, self.land = links, place, full, land
+        self.total, self.side, self.last, self.out = total, side, last, out
+        self.y_id = links.recv_ids(4)
+        self.ids = {n: links.recv_ids() for n in ("la", "lr", "ra", "rr", "lc", "rc", "core")}
+        self.active = place.c == place.y // 2
+
+    def begin(self):
+        place = self.place
+        for low in range(2):
+            y = 2 * place.c + low
+            self.links.send(
+                self.full.at[:, pl.ds(2 * low, 2)],
+                self.land.at[place.y],
+                place.device(place.x, y, place.z, place.c),
+                self.y_id + place.y,
+                when=y != place.y,
+            )
+
+    def cross(self):
+        place, links, side, active = self.place, self.links, self.side, self.active
+        x = place.x
+        for k in range(1, 4):
+            y = (place.y + k) % 4
+            links.wait(
+                self.land.at[y], place.device(x, y, place.z, place.c), self.y_id + y, when=active
+            )
+
+        @pl.when(active)
+        def _():
+            def add(i, carry):
+                acc = self.full[i, pl.ds((place.y % 2) * 2, 2)].astype(F32)
+                for k in range(1, 4):
+                    acc = acc + self.land[(place.y + k) % 4, i].astype(F32)
+                self.total[i] = acc.astype(BF)
+                return carry
+
+            lax.fori_loop(0, 4, add, 0)
+
+        self.ring()
+
+    def ring(self):
+        links, place, active, side, x = self.links, self.place, self.active, self.side, self.place.x
+        total, ids = self.total, self.ids
+        links.send(total.at[(x + 2) % 4, 0], side.at[0], place.right_x, ids["la"], when=active)
+        links.send(total.at[(x + 2) % 4, 1], side.at[2], place.left_x, ids["ra"], when=active)
+        links.send(total.at[(x + 1) % 4, 1], side.at[1], place.right_x, ids["lr"], when=active)
+        links.send(total.at[(x + 3) % 4, 0], side.at[3], place.left_x, ids["rr"], when=active)
+
+    def relay(self):
+        place, links, side, ids, active = self.place, self.links, self.side, self.ids, self.active
+        x = place.x
+        links.wait(side.at[0], place.left_x, ids["la"], when=active)
+        links.wait(side.at[2], place.right_x, ids["ra"], when=active)
+
+        @pl.when(active)
+        def _():
+            side[6] = (self.total[(x + 1) % 4, 0].astype(F32) + side[0].astype(F32)).astype(BF)
+            side[7] = (self.total[(x + 3) % 4, 1].astype(F32) + side[2].astype(F32)).astype(BF)
+
+        links.send(side.at[6], side.at[4], place.right_x, ids["lc"], when=active)
+        links.send(side.at[7], side.at[5], place.left_x, ids["rc"], when=active)
+
+    def spread(self):
+        place, links, side, ids, active = self.place, self.links, self.side, self.ids, self.active
+        x = place.x
+        links.wait(side.at[1], place.left_x, ids["lr"], when=active)
+        links.wait(side.at[3], place.right_x, ids["rr"], when=active)
+        links.wait(side.at[4], place.left_x, ids["lc"], when=active)
+        links.wait(side.at[5], place.right_x, ids["rc"], when=active)
+
+        self.deliver(((4, 3), (5, 1)))
+
+    def deliver(self, slots):
+        place, links, side, ids, active = self.place, self.links, self.side, self.ids, self.active
+        x = place.x
+
+        @pl.when(active)
+        def _():
+            sums = []
+            for half in range(2):
+                total = self.total[x, half].astype(F32)
+                for slot in slots[half]:
+                    total = total + side[slot].astype(F32)
+                sums.append(total)
+            zero, one = sums
+            self.out[...] = jnp.where(place.c == 0, zero, one)
+            side[8] = jnp.where(place.c == 0, one, zero).astype(BF)
+
+        links.send(side.at[8], self.last, place.core, ids["core"], when=active)
+
+    def finish(self):
+        idle = jnp.logical_not(self.active)
+        self.links.wait(self.last, self.place.core, self.ids["core"], when=idle)
+
+        @pl.when(idle)
+        def _():
+            self.out[...] = self.last[...].astype(F32)
+
+
+class WeightSumYDirect(WeightSumY):
+    def ring(self):
+        place = self.place
+        for k, name in ((2, "ra"), (1, "la"), (3, "lr")):
+            self.links.send(
+                self.total.at[(place.x + k) % 4],
+                self.side.at[pl.ds(2 * (k - 1), 2)],
+                place.at(dx=k),
+                self.ids[name],
+                when=self.active,
+            )
+
+    def spread(self):
+        for k, name in ((1, "la"), (3, "lr"), (2, "ra")):
+            self.links.wait(
+                self.side.at[pl.ds(2 * (k - 1), 2)],
+                self.place.at(dx=4 - k),
+                self.ids[name],
+                when=self.active,
+            )
+        self.deliver(((0, 2, 4), (1, 3, 5)))
+
+
 def token_rows(c, z, by_z):
     index = z * 2 + c if by_z else c * 4 + z
     return pl.multiple_of(index * TOK, TOK)
@@ -265,21 +472,29 @@
     def half(self, z, h):
         return pl.ds(token_rows(self.place.c, z, self.by_z) + 64 * h, 64)
 
-    def cross(self, k):
-        place, links, side = self.place, self.links, self.side
+    def cross(self, k, when=None):
+        place, links, side, ids = self.place, self.links, self.side, self.ids
         z = (place.z + k) % 4
-        links.wait(self.core_in.at[z], place.core, self.core_id + z)
-        rows = self.rows(place.c, z)
-        self.partial[rows] = (
-            self.partial[rows].astype(F32) + self.core_in[z].astype(F32)
-        ).astype(BF)
+        links.wait(self.core_in.at[z], place.core, self.core_id + z, when=when)
+
+        def add():
+            rows = self.rows(place.c, z)
+            self.partial[rows] = (
+                self.partial[rows].astype(F32) + self.core_in[z].astype(F32)
+            ).astype(BF)
+
+        if when is None:
+            add()
+        else:
+            pl.when(when)(add)
+        low, high = self.partial.at[self.half(z, 0)], self.partial.at[self.half(z, 1)]
         if k == 2:
-            links.send(self.partial.at[self.half(z, 0)], side.at[0], place.right_z, self.ids["la"])
-            links.send(self.partial.at[self.half(z, 1)], side.at[2], place.left_z, self.ids["ra"])
+            links.send(low, side.at[0], place.right_z, ids["la"], when=when)
+            links.send(high, side.at[2], place.left_z, ids["ra"], when=when)
         if k == 1:
-            links.send(self.partial.at[self.half(z, 1)], side.at[1], place.right_z, self.ids["lr"])
+            links.send(high, side.at[1], place.right_z, ids["lr"], when=when)
         if k == 3:
-            links.send(self.partial.at[self.half(z, 0)], side.at[3], place.left_z, self.ids["rr"])
+            links.send(low, side.at[3], place.left_z, ids["rr"], when=when)
 
     def relay(self):
         place, links, side = self.place, self.links, self.side
@@ -310,7 +525,7 @@
 class TokenGather:
     def __init__(self, links, place, buf, by_z):
         self.links, self.place, self.buf, self.by_z = links, place, buf, by_z
-        names = ("zm", "zp", "l", "r", "c0", "c1", "c2", "c3")
+        names = ("zm0", "zm1", "zp0", "zp1", "l", "r", "c0", "c1", "c2", "c3")
         self.ids = {name: links.recv_ids() for name in names}
 
     def rows(self, k, core=0, half=None):
@@ -324,18 +539,22 @@
         self.links.send(ref, ref, device, self.ids[name])
 
     def begin(self):
-        place, own = self.place, self.rows(0)
-        self.push(own, place.right_z, "zm")
-        self.push(own, place.left_z, "zp")
-        self.push(own, place.core, "c0")
+        place = self.place
+        self.push(self.rows(0, half=0), place.right_z, "zm0")
+        self.push(self.rows(0, half=1), place.left_z, "zp1")
+        self.push(self.rows(0), place.core, "c0")
+        self.push(self.rows(0, half=1), place.right_z, "zm1")
+        self.push(self.rows(0, half=0), place.left_z, "zp0")
 
     def sides(self):
-        place = self.place
-        self.links.wait(self.rows(3), place.left_z, self.ids["zm"])
+        place, links, ids = self.place, self.links, self.ids
+        links.wait(self.rows(3, half=0), place.left_z, ids["zm0"])
         self.push(self.rows(3, half=0), place.right_z, "l")
+        links.wait(self.rows(1, half=1), place.right_z, ids["zp1"])
+        self.push(self.rows(1, half=1), place.left_z, "r")
+        links.wait(self.rows(3, half=1), place.left_z, ids["zm1"])
         self.push(self.rows(3), place.core, "c3")
-        self.links.wait(self.rows(1), place.right_z, self.ids["zp"])
-        self.push(self.rows(1, half=1), place.left_z, "r")
+        links.wait(self.rows(1, half=0), place.right_z, ids["zp0"])
         self.push(self.rows(1), place.core, "c1")
 
     def far(self):
@@ -349,29 +568,40 @@
 
 
 def layer_kernel(
-    wq_own,
-    wo_own,
-    wm_own,
+    w_query,
+    w_key,
+    w_value,
+    w_out,
+    w_gate,
+    w_up,
+    w_down,
     gain_own,
     x_own,
     og_own,
-    query_gain,
-    key_gain,
-    trig_own,
-    starts_own,
+    query_gain_in,
+    key_gain_in,
+    lengths_own,
+    frequency,
     out_ref,
     in_grad_ref,
     gq_ref,
+    gk_ref,
     go_ref,
-    gm_ref,
+    gu_ref,
+    gd_ref,
     gains_ref,
+    wq_own,
+    wu_own,
+    wo_stage,
+    wd_stage,
     wq,
+    wu,
     wo,
-    wm,
+    wd,
     gain_in,
     gain_one,
     gain_two,
-    trig,
+    lengths,
     starts,
     cosine,
     sine,
@@ -384,7 +614,8 @@
     k_rot,
     vals,
     mixed,
-    lse,
+    probs_low,
+    probs_high,
     p1,
     p1_core,
     p1_side,
@@ -407,15 +638,27 @@
     p3,
     p3_core,
     p3_side,
-    gm_full,
-    gm_side,
-    gm_land,
+    gu_full,
+    gu_side,
+    gu_land,
     gq_full,
     gq_side,
     gq_land,
+    gk_full,
+    gk_land,
+    gk_total,
+    gk_side,
+    gk_last,
     go_full,
+    go_land,
+    go_total,
     go_side,
-    go_land,
+    go_last,
+    gd_full,
+    gd_land,
+    gd_total,
+    gd_side,
+    gd_last,
     out_tmp,
     in_grad_tmp,
     gg,
@@ -446,8 +689,9 @@
         pl.semaphore_signal(barrier, inc=1, device_id=peer, device_id_type=MESH)
 
     gather_q = WeightGather(links, place, wq_own, wq)
-    gather_o = WeightGather(links, place, wo_own, wo)
-    gather_m = WeightGather(links, place, wm_own, wm)
+    gather_u = WeightGather(links, place, wu_own, wu)
+    gather_o = WeightGatherX(links, place, w_out, wo_stage, wo)
+    gather_d = WeightGatherX(links, place, w_down, wd_stage, wd)
     gather_x = TokenGather(links, place, xs, False)
     gather_og = TokenGather(links, place, ogs, True)
     gather_h2 = TokenGather(links, place, h2, True)
@@ -456,10 +700,12 @@
     sum_2 = TokenSum(links, place, p2, p2_core, p2_side, True)
     sum_o = TokenSum(links, place, po, po_core, po_side, True)
     sum_3 = TokenSum(links, place, p3, p3_core, p3_side, False)
-    weight_m = WeightSum(links, place, gm_full, gm_side, gm_land, gm_ref)
-    weight_q = WeightSum(links, place, gq_full, gq_side, gq_land, gq_ref)
-    weight_o = WeightSum(links, place, go_full, go_side, go_land, go_ref)
-    x_id, og_id, trig_id, starts_id, out_id, in_grad_id = [links.recv_ids() for _ in range(6)]
+    weight_u = WeightSum(links, place, gu_full, gu_side, gu_land, gu_ref)
+    weight_q = WeightSumDirect(links, place, gq_full, gq_side, gq_land, gq_ref)
+    weight_k = WeightSumYDirect(links, place, gk_full, gk_land, gk_total, gk_side, gk_last, gk_ref)
+    weight_o = WeightSumY(links, place, go_full, go_land, go_total, go_side, go_last, go_ref)
+    weight_d = WeightSumY(links, place, gd_full, gd_land, gd_total, gd_side, gd_last, gd_ref)
+    x_id, og_id, lengths_id, out_id, in_grad_id = [links.recv_ids() for _ in range(5)]
     gain_id, gain_x_id = links.recv_ids(4), links.recv_ids(4)
     gg_y_id, gg_x_id, gg_z_id = links.recv_ids(8), links.recv_ids(4), links.recv_ids(4)
 
@@ -467,25 +713,32 @@
     def _():
         xs[own] = x_own[...]
         ogs[own_z] = og_own[...]
-        trig[...] = trig_own[...]
-        starts[...] = starts_own[...]
-
-    gain_in[place.d] = gain_own[...]
+        lengths[...] = lengths_own[...]
+
+    wq_own[:, 0:256] = w_query[...]
+    wq_own[:, 256:384] = w_key[...]
+    wq_own[:, 384:512] = w_value[...]
+    wu_own[:, 0:384] = w_gate[...]
+    wu_own[:, 384:768] = w_up[...]
+    gain_in[place.d] = jnp.broadcast_to(gain_own[...], (8, 128))
+    query_gain, key_gain = query_gain_in[...].astype(F32), key_gain_in[...].astype(F32)
 
     pl.semaphore_wait(barrier, 13)
 
     links.send(x_own, xs.at[swap_own], place.swap, x_id, when=away)
+    gather_o.begin()
+    gather_d.begin()
     gather_q.begin()
     for dy, dc in ((0, 1), (1, 0), (1, 1)):
         other_y = (y // 2) * 2 + (y % 2 + dy) % 2
         peer = place.device(x, other_y, z, (c + dc) % 2)
         links.send(gain_in.at[place.d], gain_in.at[place.d], peer, gain_id + place.d % 4)
-    links.send(trig_own, trig, place.core, trig_id, when=home)
-    links.send(starts_own, starts, place.core, starts_id, when=home)
-    gather_o.begin()
+    links.send(lengths_own, lengths, place.core, lengths_id, when=home)
 
     links.wait(xs.at[own], place.swap, x_id, when=away)
     gather_x.begin()
+    gather_o.relay()
+    gather_d.relay()
     gather_q.second()
     for dy, dc in ((0, 1), (1, 0), (1, 1)):
         other_y = (y // 2) * 2 + (y % 2 + dy) % 2
@@ -495,12 +748,13 @@
     four = pl.ds(x * 4, 4)
     for k in range(1, 4):
         links.send(gain_in.at[four], gain_in.at[four], place.at(dx=k), gain_x_id + x)
-    gather_o.second()
     links.send(og_own, ogs.at[swap_z], place.swap, og_id, when=away)
+    gather_o.spread()
+    gather_u.begin()
 
     gather_x.sides()
     gather_q.third()
-    gather_m.begin()
+    gather_d.spread()
     for k in range(1, 4):
         other = (x + k) % 4
         links.wait(gain_in.at[pl.ds(other * 4, 4)], place.at(dx=k), gain_x_id + other)
@@ -511,26 +765,27 @@
         gain_one[0:1, cols] = jnp.where(low, even, pltpu.roll(odd, 64, 1))
         gain_two[0:1, cols] = jnp.where(low, pltpu.roll(even, 64, 1), odd)
 
-    links.wait(trig, place.core, trig_id, when=away)
-    links.wait(starts, place.core, starts_id, when=away)
+    links.wait(lengths, place.core, lengths_id, when=away)
 
     def trig_chunk(i, carry):
         rows = pl.ds(pl.multiple_of(i * CH, CH), CH)
-        pair = trig[rows]
-        turned = pltpu.roll(pair, 64, 1)
-        cosine[rows] = jnp.where(low, pair, turned)
-        sine[rows] = jnp.where(low, -turned, pair)
+        at = lax.broadcasted_iota(jnp.int32, (CH, 1), 0) + i * CH
+        end, start = jnp.zeros((1, 1), jnp.int32), jnp.zeros((CH, 1), jnp.int32)
+        for k in range(3):
+            end = end + lengths[0:1, k : k + 1]
+            start = jnp.where(at >= end, end, start)
+        starts[rows] = start
+        angles = (at - start).astype(F32) * frequency[0:1]
+        cosine[rows] = jnp.cos(angles)
+        turned = jnp.sin(angles)
+        sine[rows] = jnp.where(low, -turned, turned)
         return carry
 
     lax.fori_loop(0, 4, trig_chunk, 0)
 
     gather_x.far()
-    gather_o.third()
     for k in range(4):
         gather_x.core(k)
-    links.wait(ogs.at[own_z], place.swap, og_id, when=away)
-    gather_og.begin()
-
     def norm_chunk(i, carry):
         rows = pl.ds(pl.multiple_of(i * 128, 128), 128)
         wide = xs[rows].astype(F32)
@@ -540,8 +795,9 @@
         return carry
 
     lax.fori_loop(0, 8, norm_chunk, 0)
+    links.wait(ogs.at[own_z], place.swap, og_id, when=away)
+    gather_og.begin()
     gather_q.finish()
-    gather_m.second()
 
     def qkv_chunk(i, carry):
         rows = pl.ds(pl.multiple_of(i * CH, CH), CH)
@@ -552,7 +808,7 @@
         for h in range(3):
             part = pre[:, 128 * h : 128 * h + 128]
             r = lax.rsqrt(jnp.mean(part * part, axis=-1, keepdims=True) + EPS)
-            scaled = part * r * (query_gain if h < 2 else key_gain)[0:1]
+            scaled = part * r * (query_gain if h < 2 else key_gain)
             turned = (scaled * cos + pltpu.roll(scaled, 64, 1) * sin).astype(BF)
             if h < 2:
                 q_rot[h, rows] = turned
@@ -561,6 +817,7 @@
         return carry
 
     lax.fori_loop(0, 4, qkv_chunk, 0)
+    gather_u.second()
     gather_o.finish()
     gather_og.sides()
 
@@ -568,6 +825,12 @@
         key_at = lax.broadcasted_iota(jnp.int32, (CH, keys), 1)
         query_at = lax.broadcasted_iota(jnp.int32, (CH, keys), 0) + qb * CH
         return (key_at >= starts[qb * CH : qb * CH + CH]) & (key_at <= query_at)
+
+    def probs_of(qb):
+        return probs_low if qb < 2 else probs_high
+
+    def probs_rows(qb):
+        return slice((qb % 2) * CH, (qb % 2) * CH + CH)
 
     def send_chunk(group_sum, qb):
         for b in (2 * qb, 2 * qb + 1):
@@ -582,40 +845,43 @@
             top = jnp.max(scores, axis=-1, keepdims=True)
             terms = jnp.exp(scores - top)
             total = jnp.sum(terms, axis=-1, keepdims=True)
-            lse[h, rows] = top + jnp.log(total)
             weights = (terms * (1.0 / total)).astype(BF)
+            probs_of(qb)[h, probs_rows(qb), 0:keys] = weights
             mixed[rows, 128 * h : 128 * h + 128] = dot(weights, vals[0:keys]).astype(BF)
-        p1[rows] = dot_nt(mixed[rows], wo[...]).astype(BF)
+        p1[rows] = dot_nt(mixed[rows], wo[...].reshape(WIDTH, 256)).astype(BF)
         send_chunk(sum_1, qb)
-        if qb == 1:
-            gather_m.third()
-
-    for k in (2, 1, 3, 0):
-        sum_1.cross(k)
+        if qb == 2:
+            for k in (2, 1, 3):
+                sum_1.cross(k, when=c == 0)
+
+    for k in (2, 1, 3):
+        sum_1.cross(k, when=c == 1)
+    sum_1.cross(0)
+    gather_u.third()
     gather_og.far()
     sum_1.relay()
-    gather_m.finish()
-    for k in range(4):
-        gather_og.core(k)
-
-    def grad_act_chunk(i, carry):
-        rows = pl.ds(pl.multiple_of(i * CH, CH), CH)
-        grad_act[rows] = dot(ogs[rows], wm[:, 768:1152])
-        return carry
-
-    lax.fori_loop(0, 4, grad_act_chunk, 0)
 
     mid = xs[own].astype(F32) + sum_1.total()
     middle[...] = mid
     r_two = lax.rsqrt(jnp.mean(mid * mid, axis=-1, keepdims=True) + EPS)
     h2[own_z] = (mid * r_two * gain_two[0:1]).astype(BF)
     gather_h2.begin()
+    gather_d.finish()
+    for k in range(4):
+        gather_og.core(k)
+
+    def grad_act_chunk(i, carry):
+        rows = pl.ds(pl.multiple_of(i * CH, CH), CH)
+        grad_act[rows] = dot(ogs[rows], wd[...].reshape(WIDTH, 384))
+        return carry
+
+    lax.fori_loop(0, 4, grad_act_chunk, 0)
 
     def mlp_chunk(k):
         gather_h2.core(k)
         at = (z + k) % 4
         rows = pl.ds(pl.multiple_of(at * CH, CH), CH)
-        pre = dot(h2[rows], wm[:, 0:768])
+        pre = dot(h2[rows], wu[...])
         gate, up = pre[:, 0:384], pre[:, 384:768]
         sig = 1.0 / (1.0 + jnp.exp(-gate))
         silu = gate * sig
@@ -624,14 +890,15 @@
         grad = grad_act[rows]
         dgu[rows, 0:384] = (grad * up * (sig * (1.0 + gate * (1.0 - sig)))).astype(BF)
         dgu[rows, 384:768] = (grad * silu).astype(BF)
-        p2[rows] = dot_nt(dgu[rows], wm[:, 0:768]).astype(BF)
+        p2[rows] = dot_nt(dgu[rows], wu[...]).astype(BF)
         sum_2.send_core(at)
 
     def down_chunk(i, carry):
         rows = pl.ds(pl.multiple_of(i * CH, CH), CH)
-        po[rows] = dot_nt(act[rows], wm[:, 768:1152]).astype(BF)
+        po[rows] = dot_nt(act[rows], wd[...].reshape(WIDTH, 384)).astype(BF)
         return carry
 
+    gather_u.finish()
     mlp_chunk(0)
     gather_h2.sides()
     mlp_chunk(3)
@@ -650,12 +917,13 @@
 
     def mlp_weight_chunk(i, carry):
         cols = pl.ds(pl.multiple_of(i * CH, CH), CH)
-        gm_full[cols, 0:768] = dot_tn(h2[:, cols], dgu[...]).astype(BF)
-        gm_full[cols, 768:1152] = dot_tn(ogs[:, cols], act[...]).astype(BF)
+        gu_full[cols] = dot_tn(h2[:, cols], dgu[...]).astype(BF)
+        gd_full[i] = dot_tn(ogs[:, cols], act[...]).astype(BF).reshape(4, 64, 384)
         return carry
 
     lax.fori_loop(0, 4, mlp_weight_chunk, 0)
-    weight_m.begin()
+    weight_u.begin()
+    weight_d.begin()
 
     err = sum_2.total()
     mid = middle[...]
@@ -677,14 +945,15 @@
     gather_gb.sides()
     for k in (2, 1, 3, 0):
         sum_o.cross(k)
-    weight_m.relay()
+    weight_u.relay()
+    weight_d.cross()
     gather_gb.far()
     for k in range(4):
         gather_gb.core(k)
 
     def out_weight_chunk(i, carry):
         cols = pl.ds(pl.multiple_of(i * CH, CH), CH)
-        go_full[cols] = dot_tn(gb[:, cols], mixed[...]).astype(BF)
+        go_full[i] = dot_tn(gb[:, cols], mixed[...]).astype(BF).reshape(4, 64, 256)
         return carry
 
     def back_rope(turned, pre, gain, cos, sin):
@@ -695,29 +964,31 @@
         grad = r * (scaled - normed * jnp.mean(scaled * normed, axis=-1, keepdims=True))
         return grad, jnp.sum(err * normed, axis=0, keepdims=True)
 
+    lax.fori_loop(0, 4, out_weight_chunk, 0)
+    weight_o.begin()
+
     attn_part = jnp.zeros((1, WIDTH), F32)
     for qb in (3, 2, 1, 0):
         rows = slice(qb * CH, qb * CH + CH)
         keys = CH * (qb + 1)
-        ok = allowed(qb, keys)
         cos, sin = cosine[rows], sine[rows]
-        grad_mixed = dot(gb[rows], wo[...]).astype(BF)
+        grad_mixed = dot(gb[rows], wo[...].reshape(WIDTH, 256)).astype(BF)
         for h in range(2):
             grad_h = grad_mixed[:, 128 * h : 128 * h + 128]
-            scores = jnp.where(ok, dot_nt(q_rot[h, rows], k_rot[0:keys]) * SCALE, MASKED)
-            probs = jnp.exp(scores - lse[h, rows])
+            weights = probs_of(qb)[h, probs_rows(qb), 0:keys]
+            wide = weights.astype(F32)
             grad_probs = dot_nt(grad_h, vals[0:keys])
-            inner = jnp.sum(probs * grad_probs, axis=-1, keepdims=True)
-            grad_scores = (probs * (grad_probs - inner)).astype(BF)
+            inner = jnp.sum(wide * grad_probs, axis=-1, keepdims=True)
+            grad_scores = (wide * (grad_probs - inner)).astype(BF)
             dk[0:keys] += dot_tn(grad_scores, q_rot[h, rows]) * SCALE
-            dv[0:keys] += dot_tn(probs.astype(BF), grad_h)
+            dv[0:keys] += dot_tn(weights, grad_h)
             grad_q = (dot(grad_scores, k_rot[0:keys]) * SCALE).astype(BF).astype(F32)
             pre = qk_pre[rows, 128 * h : 128 * h + 128]
-            grad, gain_part = back_rope(grad_q, pre, query_gain[0:1], cos, sin)
+            grad, gain_part = back_rope(grad_q, pre, query_gain, cos, sin)
             dqkv[rows, 128 * h : 128 * h + 128] = grad.astype(BF)
             gg[16:17] += gain_part
         grad_k = dk[rows].astype(BF).astype(F32)
-        grad, gain_part = back_rope(grad_k, qk_pre[rows, 256:384], key_gain[0:1], cos, sin)
+        grad, gain_part = back_rope(grad_k, qk_pre[rows, 256:384], key_gain, cos, sin)
         dqkv[rows, 256:384] = grad.astype(BF)
         gg[17:18] += gain_part
         dqkv[rows, 384:512] = dv[rows].astype(BF)
@@ -727,11 +998,21 @@
         attn_part += jnp.sum(err * (xs[rows].astype(F32) * r1[rows]), axis=0, keepdims=True)
         if qb == 3:
             sum_o.relay()
+            weight_d.relay()
         if qb == 2:
-            weight_m.spread()
-
-    for k in (2, 1, 3, 0):
-        sum_3.cross(k)
+            weight_u.spread()
+            weight_o.cross()
+        if qb == 1:
+            for k in (2, 1, 3):
+                sum_3.cross(k, when=c == 1)
+            weight_d.spread()
+            weight_o.relay()
+            out_tmp[...] = (middle[...] + sum_o.total()).astype(BF)
+            links.send(out_tmp, out_ref, place.swap, out_id, when=away)
+
+    for k in (2, 1, 3):
+        sum_3.cross(k, when=c == 0)
+    sum_3.cross(0)
     for k in range(8):
         gg[k : k + 1] = attn_part[:, 128 * k : 128 * k + 128]
     for dy, dc in column:
@@ -739,17 +1020,15 @@
 
     def attn_weight_chunk(i, carry):
         cols = pl.ds(pl.multiple_of(i * CH, CH), CH)
-        gq_full[cols] = dot_tn(h1[:, cols], dqkv[...]).astype(BF)
+        grad = dot_tn(h1[:, cols], dqkv[...]).astype(BF)
+        gq_full[pl.ds(2 * i, 2)] = grad[:, 0:256].reshape(2, 128, 256)
+        gk_full[i] = grad[:, 256:512].reshape(4, 64, 256)
         return carry
 
     lax.fori_loop(0, 4, attn_weight_chunk, 0)
+    weight_k.begin()
     weight_q.begin()
     sum_3.relay()
-    lax.fori_loop(0, 4, out_weight_chunk, 0)
-    weight_o.begin()
-
-    out_tmp[...] = (middle[...] + sum_o.total()).astype(BF)
-    links.send(out_tmp, out_ref, place.swap, out_id, when=away)
 
     gg_y[y * 2 + c] = gg[...]
     for dy, dc in column:
@@ -761,8 +1040,11 @@
     gg_a[...] = total
     for k in range(1, 4):
         links.send(gg_a, gg_x.at[x], place.at(dx=k), gg_x_id + x)
-    weight_q.relay()
-    weight_o.relay()
+    weight_o.spread()
+    weight_u.finish()
+    weight_d.finish()
+    weight_k.cross()
+    weight_q.spread()
 
     err = sum_3.total()
     r_one = r1[own]
@@ -782,9 +1064,8 @@
     for k in range(1, 4):
         links.send(gg_b, gg_z.at[z], place.at(dz=k), gg_z_id + z)
 
-    weight_q.spread()
-    weight_o.spread()
-    weight_m.finish()
+    weight_k.spread()
+    weight_o.finish()
 
     @pl.when(home)
     def _():
@@ -798,7 +1079,7 @@
     gains_ref[...] = (gg_z[0] + gg_z[1]) + (gg_z[2] + gg_z[3])
 
     weight_q.finish()
-    weight_o.finish()
+    weight_k.finish()
     links.wait(out_ref, place.swap, out_id, when=away)
     links.wait(in_grad_ref, place.swap, in_grad_id, when=away)
     links.drain()
@@ -822,14 +1103,28 @@
     def weight_landing(cols):
         return [buf((WIDTH, cols)), buf((10, 128, cols)), buf((4, 64, cols))]
 
+    def weight_landing_y(cols):
+        return [
+            buf((4, 4, 64, cols)),
+            buf((4, 4, 2, 64, cols)),
+            buf((4, 2, 64, cols)),
+            buf((9, 64, cols)),
+            buf((64, cols)),
+        ]
+
     scratch = [
+        buf((64, NQ)),
+        buf((64, NU)),
+        buf((4, 64, NO)),
+        buf((4, 64, ND)),
         buf((WIDTH, NQ)),
-        buf((WIDTH, NO)),
-        buf((WIDTH, NM)),
+        buf((WIDTH, NU)),
+        buf((4, 4, 64, NO)),
+        buf((4, 4, 64, ND)),
         buf((16, 8, 128), F32),
         buf((1, WIDTH), F32),
         buf((1, WIDTH), F32),
-        buf(table, F32),
+        buf((1, 4), jnp.int32),
         buf((GROUP, 1), jnp.int32),
         buf(table, F32),
         buf(table, F32),
@@ -842,7 +1137,8 @@
         buf(table),
         buf(table),
         buf((GROUP, 256)),
-        buf((2, GROUP, 1), F32),
+        buf((2, 512, 512)),
+        buf((2, 512, GROUP)),
         *landing,
         buf(block, F32),
         buf(group),
@@ -857,9 +1153,12 @@
         buf(table, F32),
         buf((GROUP, 512)),
         *landing,
-        *weight_landing(NM),
-        *weight_landing(NQ),
-        *weight_landing(NO),
+        *weight_landing(NU),
+        buf((8, 128, 256)),
+        *weight_landing(256)[1:],
+        *weight_landing_y(NO),
+        *weight_landing_y(NO),
+        *weight_landing_y(ND),
         buf(block),
         buf(block),
         buf(gains, F32),
@@ -876,13 +1175,15 @@
         out_shape=(
             sds(block, BF),
             sds(block, BF),
-            sds((64, NQ), F32),
+            sds((64, 256), F32),
+            sds((64, 256), F32),
             sds((64, NO), F32),
-            sds((64, NM), F32),
+            sds((64, NU), F32),
+            sds((64, ND), F32),
             sds(gains, F32),
         ),
         in_specs=[vmem] * len(args),
-        out_specs=(vmem,) * 6,
+        out_specs=(vmem,) * 8,
         scratch_shapes=scratch,
         name="layer",
         compiler_params=pltpu.CompilerParams(
@@ -891,18 +1192,70 @@
     )(*args)
 
 
-def tables(lengths):
-    ends = jnp.cumsum(lengths)
-    begins = ends - lengths
-    at = jnp.arange(GROUP, dtype=jnp.int32)
-    label = jnp.sum((at[:, None] >= ends[None, :]).astype(jnp.int32), axis=1)
-    chosen = label[:, None] == jnp.arange(lengths.shape[0], dtype=jnp.int32)[None, :]
-    starts = jnp.sum(jnp.where(chosen, begins[None, :], 0), axis=1)
-    half = HEAD // 2
-    frequency = ROPE_BASE ** (-(jnp.arange(half).astype(F32) * 2.0 / HEAD))
-    angles = (at - starts).astype(F32)[:, None] * frequency[None, :]
-    cos, sin = jnp.cos(angles), jnp.sin(angles)
-    return jnp.concatenate([cos, sin], axis=-1), starts[:, None]
+def results_kernel(
+    out_in,
+    in_grad_in,
+    gq,
+    gk,
+    go,
+    gu,
+    gd,
+    gains,
+    out,
+    in_grad,
+    attn_gain,
+    query,
+    key,
+    value,
+    query_gain,
+    key_gain,
+    w_out,
+    mlp_gain,
+    gate,
+    up,
+    down,
+):
+    d = lax.axis_index("dp")
+    out[...] = out_in[...]
+    in_grad[...] = in_grad_in[...]
+    query[...] = gq[...]
+    key[...] = gk[:, 0:128]
+    value[...] = gk[:, 128:256]
+    w_out[...] = go[...]
+    gate[...] = gu[:, 0:384]
+    up[...] = gu[:, 384:768]
+    down[...] = gd[...]
+    query_gain[...] = gains[16:17]
+    key_gain[...] = gains[17:18]
+    for first, ref in ((0, attn_gain), (8, mlp_gain)):
+        row = gains[pl.ds(first + d // 2, 1)]
+        ref[...] = jnp.where(d % 2 == 1, pltpu.roll(row, 64, 1), row)[:, 0:64]
+
+
+def write_results(*args):
+    vmem = pl.BlockSpec(memory_space=pltpu.VMEM)
+    shapes = [
+        ((TOK, WIDTH), BF),
+        ((TOK, WIDTH), BF),
+        ((1, 64), F32),
+        ((64, 256), F32),
+        ((64, 128), F32),
+        ((64, 128), F32),
+        ((1, 128), F32),
+        ((1, 128), F32),
+        ((64, 256), F32),
+        ((1, 64), F32),
+        ((64, 384), F32),
+        ((64, 384), F32),
+        ((64, 384), F32),
+    ]
+    return pl.pallas_call(
+        results_kernel,
+        out_shape=tuple(jax.ShapeDtypeStruct(shape, kind) for shape, kind in shapes),
+        in_specs=[vmem] * len(args),
+        out_specs=(vmem,) * len(shapes),
+        name="results",
+    )(*args)
 
 
 def per_device(
@@ -921,41 +1274,29 @@
     w_down,
     out_grad,
 ):
-    trig, starts = tables(seq_lengths[0])
-    wq_own = jnp.concatenate([w_query, key_projection, value_projection], axis=1)
-    wm_own = jnp.concatenate([w_gate, w_up, w_down.T], axis=1)
-    gain_own = jnp.broadcast_to(jnp.concatenate([attn_gain, mlp_gain]).astype(F32)[None], (8, 128))
-    out, in_grad, gq, go, gm, gains = run_layer(
-        wq_own,
+    half = HEAD // 2
+    frequency = ROPE_BASE ** (-(jnp.arange(half).astype(F32) * 2.0 / HEAD))
+    parts = run_layer(
+        w_query,
+        key_projection,
+        value_projection,
         w_out.T,
-        wm_own,
-        gain_own,
+        w_gate,
+        w_up,
+        w_down.T,
+        jnp.concatenate([attn_gain, mlp_gain]).astype(F32)[None],
         layer_input,
         out_grad,
-        query_gain.astype(F32)[None],
-        key_gain.astype(F32)[None],
-        trig,
-        starts,
+        query_gain[None],
+        key_gain[None],
+        seq_lengths,
+        jnp.concatenate([frequency, frequency])[None],
     )
-    piece = attn_gain.shape[0]
-    first = lax.axis_index("dp") * piece
-    grad_attn_gain = lax.dynamic_slice_in_dim(gains[0:8].reshape(-1), first, piece, 0)
-    grad_mlp_gain = lax.dynamic_slice_in_dim(gains[8:16].reshape(-1), first, piece, 0)
-    return (
-        out,
-        in_grad,
-        grad_attn_gain,
-        gq[:, 0:256],
-        gq[:, 256:384],
-        gq[:, 384:512],
-        gains[16],
-        gains[17],
-        go.T,
-        grad_mlp_gain,
-        gm[:, 0:384],
-        gm[:, 384:768],
-        gm[:, 768:1152].T,
-    )
+    results = list(write_results(*parts))
+    for k in (2, 6, 7, 9):
+        results[k] = results[k].reshape(-1)
+    results[8], results[12] = results[8].T, results[12].T
+    return tuple(results)
 
 
 def solution(mesh):

time: 164 us -> 137 us (0.84)
  Pallas kernels: 146 us -> 135 us
  local copies, waits for them, and re-layouts: 11 us -> 0.66 us
  other arithmetic: 5.15 us -> 1.18 us
    pallas_call x1, Pallas kernels: 146 us -> 132 us  [run_layer(): pl.pallas_call(layer_kernel, out_shape=(sds(block, BF), sds(block, BF), s...]
    unnamed x33 -> x4, local copies, waits for them, and re-layouts: 3.3 us -> 0.66 us
    concatenate x3 -> x0, other arithmetic: 2.32 us -> none  [the longest x1 1 us: tables(): return (jnp.concatenate([cos, sin], axis=-1), starts[:, None])]
    pallas_call x0 -> x1, Pallas kernels: none -> 2.22 us  [write_results(): pl.pallas_call(results_kernel, out_shape=tuple((jax.ShapeDtypeStruct(shap...]
    cos x1 -> x0, other arithmetic: 1.88 us -> none  [tables(): cos, sin = (jnp.cos(angles), jnp.sin(angles))]
    transpose x1 -> x0, local copies, waits for them, and re-layouts: 1.74 us -> none  [per_device(): gm[:, 768:1152]]
where the time goes in v3:
time: 137 us
  Pallas kernels  135 us (99%)
    pallas_call x1, Pallas kernels, run_layer(): pl.pallas_call(layer_kernel, out_shape=(sds(block, BF), sds(block, BF), s...  132 us

profile of v3, /device:TPU:1, one launch (start us, length us, event | category | flops | bytes accessed | tf_op | source)
XLA Modules:
  0.0 137.2 jit_solution(11667490447638147742)
XLA Ops:
  0.6 0.0 copy-start
  0.7 0.0 copy-start.1
  0.7 0.6 copy-done
  1.3 0.0 copy-done.1
  1.3 0.6 maximum_convert_fusion.gain_own
  1.9 0.6 maximum_bitcast_fusion.frequency
  2.5 132.3 %layer.1 = (bf16[128,1024]{1,0:T(8,128)(2,1)}, bf16[128,1024]{1,0:T(8,128)(2,1)}, f32[64,256]{1,0:T(8,128)}, f32[64,256]{1,0:T(8,128)}, f32[64,256]{1,0:T(8,128)...) custom-call(bf16[64,256]{1,0:T(8,128)(2,1)} %w_query.1, bf16[64,128]{1,0:T(8,128)(2,1)} %w_key.1, ...), custom_call_target="tpu_custom_call" | custom-call | tf_op jit(solution)/shard_map/layer/pallas_call | solution.py:1173
  134.8 2.2 %results.1 = (bf16[128,1024]{1,0:T(8,128)(2,1)}, bf16[128,1024]{1,0:T(8,128)(2,1)}, f32[1,64]{1,0:T(1,128)}, f32[64,256]{1,0:T(8,128)}, f32[64,128]{1,0:T(8,128)...) custom-call(bf16[128,1024]{1,0:T(8,128)(2,1)} %get-tuple-element.34., ...), custom_call_target="tpu_custom_call" | custom-call | tf_op jit(solution)/shard_map/results/pallas_call | solution.py:1252
  (1 shorter events, 0.0 us)
Async XLA Ops:
  0.6 0.7 copy-start
  0.7 0.7 copy-start.1

commit v4 on v3

--- a/solution.py
+++ b/solution.py
@@ -2,6 +2,7 @@
 
 import jax
 import jax.numpy as jnp
+import numpy as np
 from jax import lax
 from jax.experimental import pallas as pl
 from jax.experimental.pallas import tpu as pltpu
@@ -23,7 +24,8 @@
 NU = 768
 ND = 384
 CH = 256
-N_SEMS = 240
+N_SENDS = 101
+N_RECVS = 195
 
 
 def dot(a, b):
@@ -42,12 +44,12 @@
     def __init__(self, send_sems, recv_sems):
         self.send_sems, self.recv_sems = send_sems, recv_sems
         self.sends, self.recvs = 0, 0
-        self.pending = []
+        self.pending, self.free, self.drained = [], [], 0
 
     def recv_ids(self, count=1):
         first = self.recvs
         self.recvs += count
-        assert self.recvs <= N_SEMS
+        assert self.recvs <= N_RECVS
         return first
 
     def copy(self, src, dst, device, send_id, recv_id):
@@ -60,15 +62,22 @@
             device_id_type=MESH,
         )
 
-    def send(self, src, dst, device, recv_id, when=None):
-        copy = self.copy(src, dst, device, self.sends, recv_id)
+    def send_id(self):
+        if self.free:
+            return self.free.pop()
         self.sends += 1
-        assert self.sends <= N_SEMS
+        assert self.sends <= N_SENDS
+        return self.sends - 1
+
+    def send(self, src, dst, device, recv_id, when=None, send_id=None):
+        if send_id is None:
+            send_id = self.send_id()
+        copy = self.copy(src, dst, device, send_id, recv_id)
         if when is None:
             copy.start()
         else:
             pl.when(when)(copy.start)
-        self.pending.append((copy, when))
+        self.pending.append((copy, when, send_id))
 
     def wait(self, dst, device, recv_id, when=None):
         copy = self.copy(dst, dst, device, 0, recv_id)
@@ -77,12 +86,18 @@
         else:
             pl.when(when)(copy.wait_recv)
 
-    def drain(self):
-        for copy, when in self.pending:
+    def issued(self):
+        return self.drained + len(self.pending)
+
+    def drain(self, upto):
+        count = upto - self.drained
+        done, self.pending, self.drained = self.pending[:count], self.pending[count:], upto
+        for copy, when, _ in done:
             if when is None:
                 copy.wait_send()
             else:
                 pl.when(when)(copy.wait_send)
+        self.free += sorted({send_id for _, _, send_id in done})
 
 
 class Place:
@@ -455,6 +470,12 @@
         self.core_in, self.side, self.by_z = core_in, side, by_z
         self.core_id = links.recv_ids(4)
         self.ids = {n: links.recv_ids() for n in ("la", "lr", "ra", "rr", "lc", "rc")}
+        self.shared = {}
+
+    def send_id(self, name):
+        if name not in self.shared:
+            self.shared[name] = self.links.send_id()
+        return self.shared[name]
 
     def rows(self, c, z):
         return pl.ds(token_rows(c, z, self.by_z), TOK)
@@ -467,6 +488,7 @@
             place.core,
             self.core_id + z,
             when=when,
+            send_id=None if when is None else self.send_id(z),
         )
 
     def half(self, z, h):
@@ -488,13 +510,15 @@
         else:
             pl.when(when)(add)
         low, high = self.partial.at[self.half(z, 0)], self.partial.at[self.half(z, 1)]
-        if k == 2:
-            links.send(low, side.at[0], place.right_z, ids["la"], when=when)
-            links.send(high, side.at[2], place.left_z, ids["ra"], when=when)
-        if k == 1:
-            links.send(high, side.at[1], place.right_z, ids["lr"], when=when)
-        if k == 3:
-            links.send(low, side.at[3], place.left_z, ids["rr"], when=when)
+        for at, ref, slot, device, name in (
+            (2, low, 0, place.right_z, "la"),
+            (2, high, 2, place.left_z, "ra"),
+            (1, high, 1, place.right_z, "lr"),
+            (3, low, 3, place.left_z, "rr"),
+        ):
+            if k == at:
+                send_id = None if when is None else self.send_id(name)
+                links.send(ref, side.at[slot], device, ids[name], when=when, send_id=send_id)
 
     def relay(self):
         place, links, side = self.place, self.links, self.side
@@ -512,14 +536,25 @@
         links.wait(side.at[3], place.right_z, self.ids["rr"])
         links.wait(side.at[4], place.left_z, self.ids["lc"])
         links.wait(side.at[5], place.right_z, self.ids["rc"])
-        parts = []
-        for half, first, other in ((0, 4, 3), (1, 5, 1)):
-            parts.append(
-                self.partial[self.half(place.z, half)].astype(F32)
-                + side[first].astype(F32)
-                + side[other].astype(F32)
-            )
-        return jnp.concatenate(parts, axis=0)
+        return jnp.concatenate([self.half_sum(0), self.half_sum(1)], axis=0)
+
+    def half_sum(self, half):
+        first, other = ((4, 3), (5, 1))[half]
+        return (
+            self.partial[self.half(self.place.z, half)].astype(F32)
+            + self.side[first].astype(F32)
+            + self.side[other].astype(F32)
+        )
+
+    def half_total(self, half):
+        place, links, side = self.place, self.links, self.side
+        if half == 0:
+            links.wait(side.at[3], place.right_z, self.ids["rr"])
+            links.wait(side.at[4], place.left_z, self.ids["lc"])
+        else:
+            links.wait(side.at[1], place.left_z, self.ids["lr"])
+            links.wait(side.at[5], place.right_z, self.ids["rc"])
+        return self.half_sum(half)
 
 
 class TokenGather:
@@ -575,7 +610,8 @@
     w_gate,
     w_up,
     w_down,
-    gain_own,
+    attn_gain,
+    mlp_gain,
     x_own,
     og_own,
     query_gain_in,
@@ -632,10 +668,6 @@
     po_side,
     gb,
     grad_mid,
-    dk,
-    dv,
-    dqkv,
-    p3,
     p3_core,
     p3_side,
     gu_full,
@@ -699,13 +731,14 @@
     sum_1 = TokenSum(links, place, p1, p1_core, p1_side, False)
     sum_2 = TokenSum(links, place, p2, p2_core, p2_side, True)
     sum_o = TokenSum(links, place, po, po_core, po_side, True)
-    sum_3 = TokenSum(links, place, p3, p3_core, p3_side, False)
+    sum_3 = TokenSum(links, place, h2, p3_core, p3_side, False)
     weight_u = WeightSum(links, place, gu_full, gu_side, gu_land, gu_ref)
     weight_q = WeightSumDirect(links, place, gq_full, gq_side, gq_land, gq_ref)
     weight_k = WeightSumYDirect(links, place, gk_full, gk_land, gk_total, gk_side, gk_last, gk_ref)
     weight_o = WeightSumY(links, place, go_full, go_land, go_total, go_side, go_last, go_ref)
     weight_d = WeightSumY(links, place, gd_full, gd_land, gd_total, gd_side, gd_last, gd_ref)
-    x_id, og_id, lengths_id, out_id, in_grad_id = [links.recv_ids() for _ in range(5)]
+    x_id, og_id, lengths_id, out_id = [links.recv_ids() for _ in range(4)]
+    in_grad_id = links.recv_ids(2)
     gain_id, gain_x_id = links.recv_ids(4), links.recv_ids(4)
     gg_y_id, gg_x_id, gg_z_id = links.recv_ids(8), links.recv_ids(4), links.recv_ids(4)
 
@@ -720,7 +753,8 @@
     wq_own[:, 384:512] = w_value[...]
     wu_own[:, 0:384] = w_gate[...]
     wu_own[:, 384:768] = w_up[...]
-    gain_in[place.d] = jnp.broadcast_to(gain_own[...], (8, 128))
+    gain_in[place.d, :, 0:64] = jnp.broadcast_to(attn_gain[...].astype(F32), (8, 64))
+    gain_in[place.d, :, 64:128] = jnp.broadcast_to(mlp_gain[...].astype(F32), (8, 64))
     query_gain, key_gain = query_gain_in[...].astype(F32), key_gain_in[...].astype(F32)
 
     pl.semaphore_wait(barrier, 13)
@@ -783,20 +817,24 @@
 
     lax.fori_loop(0, 4, trig_chunk, 0)
 
-    gather_x.far()
-    for k in range(4):
-        gather_x.core(k)
-    def norm_chunk(i, carry):
-        rows = pl.ds(pl.multiple_of(i * 128, 128), 128)
+    def norm_pair(k):
+        for core in range(2):
+            norm_rows(pl.ds(token_rows((c + core) % 2, (z + k) % 4, False), TOK))
+
+    def norm_rows(rows):
         wide = xs[rows].astype(F32)
         r = lax.rsqrt(jnp.mean(wide * wide, axis=-1, keepdims=True) + EPS)
         r1[rows] = r
         h1[rows] = (wide * r * gain_one[0:1]).astype(BF)
-        return carry
-
-    lax.fori_loop(0, 8, norm_chunk, 0)
+
+    for k in (0, 3, 1):
+        gather_x.core(k)
+        norm_pair(k)
+    gather_x.far()
     links.wait(ogs.at[own_z], place.swap, og_id, when=away)
     gather_og.begin()
+    gather_x.core(2)
+    norm_pair(2)
     gather_q.finish()
 
     def qkv_chunk(i, carry):
@@ -811,7 +849,7 @@
             scaled = part * r * (query_gain if h < 2 else key_gain)
             turned = (scaled * cos + pltpu.roll(scaled, 64, 1) * sin).astype(BF)
             if h < 2:
-                q_rot[h, rows] = turned
+                q_rot[pl.ds(pl.multiple_of(i * 512 + h * CH, CH), CH)] = turned
             else:
                 k_rot[rows] = turned
         return carry
@@ -830,7 +868,7 @@
         return probs_low if qb < 2 else probs_high
 
     def probs_rows(qb):
-        return slice((qb % 2) * CH, (qb % 2) * CH + CH)
+        return slice((qb % 2) * 512, (qb % 2) * 512 + 512)
 
     def send_chunk(group_sum, qb):
         for b in (2 * qb, 2 * qb + 1):
@@ -840,14 +878,15 @@
         rows = slice(qb * CH, qb * CH + CH)
         keys = CH * (qb + 1)
         ok = allowed(qb, keys)
-        for h in range(2):
-            scores = jnp.where(ok, dot_nt(q_rot[h, rows], k_rot[0:keys]) * SCALE, MASKED)
-            top = jnp.max(scores, axis=-1, keepdims=True)
-            terms = jnp.exp(scores - top)
-            total = jnp.sum(terms, axis=-1, keepdims=True)
-            weights = (terms * (1.0 / total)).astype(BF)
-            probs_of(qb)[h, probs_rows(qb), 0:keys] = weights
-            mixed[rows, 128 * h : 128 * h + 128] = dot(weights, vals[0:keys]).astype(BF)
+        scores = dot_nt(q_rot[qb * 512 : qb * 512 + 512], k_rot[0:keys]).reshape(2, CH, keys)
+        scores = jnp.where(ok[None], scores * SCALE, MASKED)
+        terms = jnp.exp(scores - jnp.max(scores, axis=-1, keepdims=True))
+        weights = terms * (1.0 / jnp.sum(terms, axis=-1, keepdims=True))
+        weights = weights.astype(BF).reshape(512, keys)
+        probs_of(qb)[probs_rows(qb), 0:keys] = weights
+        both = dot(weights, vals[0:keys]).astype(BF)
+        mixed[rows, 0:128] = both[0:CH]
+        mixed[rows, 128:256] = both[CH:512]
         p1[rows] = dot_nt(mixed[rows], wo[...].reshape(WIDTH, 256)).astype(BF)
         send_chunk(sum_1, qb)
         if qb == 2:
@@ -861,22 +900,23 @@
     gather_og.far()
     sum_1.relay()
 
+    gather_d.finish()
+    for k in range(4):
+        gather_og.core(k)
+
+    def grad_act_chunk(i, carry):
+        rows = pl.ds(pl.multiple_of(i * CH, CH), CH)
+        grad_act[rows] = dot(ogs[rows], wd[...].reshape(WIDTH, 384))
+        return carry
+
+    lax.fori_loop(0, 4, grad_act_chunk, 0)
+
     mid = xs[own].astype(F32) + sum_1.total()
     middle[...] = mid
     r_two = lax.rsqrt(jnp.mean(mid * mid, axis=-1, keepdims=True) + EPS)
     h2[own_z] = (mid * r_two * gain_two[0:1]).astype(BF)
+    before_h2 = links.issued()
     gather_h2.begin()
-    gather_d.finish()
-    for k in range(4):
-        gather_og.core(k)
-
-    def grad_act_chunk(i, carry):
-        rows = pl.ds(pl.multiple_of(i * CH, CH), CH)
-        grad_act[rows] = dot(ogs[rows], wd[...].reshape(WIDTH, 384))
-        return carry
-
-    lax.fori_loop(0, 4, grad_act_chunk, 0)
-
     def mlp_chunk(k):
         gather_h2.core(k)
         at = (z + k) % 4
@@ -906,6 +946,7 @@
     sum_2.cross(3)
     sum_2.cross(1)
     gather_h2.far()
+    after_h2 = links.issued()
     mlp_chunk(2)
     sum_2.cross(2)
     sum_2.cross(0)
@@ -925,6 +966,7 @@
     weight_u.begin()
     weight_d.begin()
 
+    links.drain(before_h2)
     err = sum_2.total()
     mid = middle[...]
     r_two = lax.rsqrt(jnp.mean(mid * mid, axis=-1, keepdims=True) + EPS)
@@ -939,17 +981,18 @@
     )
     grad_mid[...] = grad
     gb[own] = grad.astype(BF)
+    before_gb = links.issued()
     gather_gb.begin()
-    dk[...] = jnp.zeros_like(dk)
-    dv[...] = jnp.zeros_like(dv)
+    dk, dv, dqkv = grad_act.at[:, 0:128], grad_act.at[:, 128:256], dgu.at[:, 0:512]
+    grad_act[:, 0:256] = jnp.zeros((GROUP, 256), F32)
     gather_gb.sides()
-    for k in (2, 1, 3, 0):
-        sum_o.cross(k)
     weight_u.relay()
     weight_d.cross()
     gather_gb.far()
     for k in range(4):
         gather_gb.core(k)
+    for k in (2, 1, 3, 0):
+        sum_o.cross(k)
 
     def out_weight_chunk(i, carry):
         cols = pl.ds(pl.multiple_of(i * CH, CH), CH)
@@ -968,23 +1011,25 @@
     weight_o.begin()
 
     attn_part = jnp.zeros((1, WIDTH), F32)
+    p3 = h2
+    links.drain(after_h2)
     for qb in (3, 2, 1, 0):
         rows = slice(qb * CH, qb * CH + CH)
         keys = CH * (qb + 1)
         cos, sin = cosine[rows], sine[rows]
         grad_mixed = dot(gb[rows], wo[...].reshape(WIDTH, 256)).astype(BF)
+        grad_h = jnp.concatenate([grad_mixed[:, 0:128], grad_mixed[:, 128:256]], axis=0)
+        weights = probs_of(qb)[probs_rows(qb), 0:keys]
+        wide = weights.astype(F32)
+        grad_probs = dot_nt(grad_h, vals[0:keys])
+        inner = jnp.sum(wide * grad_probs, axis=-1, keepdims=True)
+        grad_scores = (wide * (grad_probs - inner)).astype(BF)
+        dk[0:keys] += dot_tn(grad_scores, q_rot[qb * 512 : qb * 512 + 512]) * SCALE
+        dv[0:keys] += dot_tn(weights, grad_h)
+        grad_q = (dot(grad_scores, k_rot[0:keys]) * SCALE).astype(BF).astype(F32)
         for h in range(2):
-            grad_h = grad_mixed[:, 128 * h : 128 * h + 128]
-            weights = probs_of(qb)[h, probs_rows(qb), 0:keys]
-            wide = weights.astype(F32)
-            grad_probs = dot_nt(grad_h, vals[0:keys])
-            inner = jnp.sum(wide * grad_probs, axis=-1, keepdims=True)
-            grad_scores = (wide * (grad_probs - inner)).astype(BF)
-            dk[0:keys] += dot_tn(grad_scores, q_rot[h, rows]) * SCALE
-            dv[0:keys] += dot_tn(weights, grad_h)
-            grad_q = (dot(grad_scores, k_rot[0:keys]) * SCALE).astype(BF).astype(F32)
             pre = qk_pre[rows, 128 * h : 128 * h + 128]
-            grad, gain_part = back_rope(grad_q, pre, query_gain, cos, sin)
+            grad, gain_part = back_rope(grad_q[CH * h : CH * h + CH], pre, query_gain, cos, sin)
             dqkv[rows, 128 * h : 128 * h + 128] = grad.astype(BF)
             gg[16:17] += gain_part
         grad_k = dk[rows].astype(BF).astype(F32)
@@ -997,9 +1042,9 @@
         send_chunk(sum_3, qb)
         attn_part += jnp.sum(err * (xs[rows].astype(F32) * r1[rows]), axis=0, keepdims=True)
         if qb == 3:
-            sum_o.relay()
             weight_d.relay()
         if qb == 2:
+            sum_o.relay()
             weight_u.spread()
             weight_o.cross()
         if qb == 1:
@@ -1007,14 +1052,15 @@
                 sum_3.cross(k, when=c == 1)
             weight_d.spread()
             weight_o.relay()
-            out_tmp[...] = (middle[...] + sum_o.total()).astype(BF)
-            links.send(out_tmp, out_ref, place.swap, out_id, when=away)
+            links.drain(before_gb)
 
     for k in (2, 1, 3):
         sum_3.cross(k, when=c == 0)
     sum_3.cross(0)
     for k in range(8):
         gg[k : k + 1] = attn_part[:, 128 * k : 128 * k + 128]
+    out_tmp[...] = (middle[...] + sum_o.total()).astype(BF)
+    links.send(out_tmp, out_ref, place.swap, out_id, when=away)
     for dy, dc in column:
         links.send(gg, gg_y.at[y * 2 + c], place.at(dy=dy, dc=dc), gg_y_id + y * 2 + c)
 
@@ -1046,15 +1092,20 @@
     weight_k.cross()
     weight_q.spread()
 
-    err = sum_3.total()
-    r_one = r1[own]
-    normed = xs[own].astype(F32) * r_one
-    scaled = err * gain_one[0:1]
-    in_grad_tmp[...] = (
-        grad_mid[...]
-        + r_one * (scaled - normed * jnp.mean(scaled * normed, axis=-1, keepdims=True))
-    ).astype(BF)
-    links.send(in_grad_tmp, in_grad_ref, place.swap, in_grad_id, when=away)
+    for half in range(2):
+        part = pl.ds(64 * half, 64)
+        mine = pl.ds(token_rows(c, z, False) + 64 * half, 64)
+        err = sum_3.half_total(half)
+        r_one = r1[mine]
+        normed = xs[mine].astype(F32) * r_one
+        scaled = err * gain_one[0:1]
+        in_grad_tmp[part] = (
+            grad_mid[part]
+            + r_one * (scaled - normed * jnp.mean(scaled * normed, axis=-1, keepdims=True))
+        ).astype(BF)
+        links.send(
+            in_grad_tmp.at[part], in_grad_ref.at[part], place.swap, in_grad_id + half, when=away
+        )
 
     gg_x[x] = gg_a[...]
     for k in range(1, 4):
@@ -1081,8 +1132,10 @@
     weight_q.finish()
     weight_k.finish()
     links.wait(out_ref, place.swap, out_id, when=away)
-    links.wait(in_grad_ref, place.swap, in_grad_id, when=away)
-    links.drain()
+    for half in range(2):
+        part = in_grad_ref.at[pl.ds(64 * half, 64)]
+        links.wait(part, place.swap, in_grad_id + half, when=away)
+    links.drain(links.issued())
 
 
 def run_layer(*args):
@@ -1133,12 +1186,12 @@
         buf(group),
         buf((GROUP, 1), F32),
         buf((GROUP, 384), F32),
-        buf((2, GROUP, HEAD)),
+        buf((2 * GROUP, HEAD)),
         buf(table),
         buf(table),
         buf((GROUP, 256)),
-        buf((2, 512, 512)),
-        buf((2, 512, GROUP)),
+        buf((GROUP, 512)),
+        buf((GROUP, GROUP)),
         *landing,
         buf(block, F32),
         buf(group),
@@ -1149,10 +1202,7 @@
         *landing,
         buf(group),
         buf(block, F32),
-        buf(table, F32),
-        buf(table, F32),
-        buf((GROUP, 512)),
-        *landing,
+        *landing[1:],
         *weight_landing(NU),
         buf((8, 128, 256)),
         *weight_landing(256)[1:],
@@ -1167,8 +1217,8 @@
         buf((4, *gains), F32),
         buf(gains, F32),
         buf((4, *gains), F32),
-        pltpu.SemaphoreType.DMA((N_SEMS,)),
-        pltpu.SemaphoreType.DMA((N_SEMS,)),
+        pltpu.SemaphoreType.DMA((N_SENDS,)),
+        pltpu.SemaphoreType.DMA((N_RECVS,)),
     ]
     return pl.pallas_call(
         layer_kernel,
@@ -1274,8 +1324,7 @@
     w_down,
     out_grad,
 ):
-    half = HEAD // 2
-    frequency = ROPE_BASE ** (-(jnp.arange(half).astype(F32) * 2.0 / HEAD))
+    frequency = ROPE_BASE ** (-(np.arange(HEAD // 2) * 2.0 / HEAD)).astype(np.float32)
     parts = run_layer(
         w_query,
         key_projection,
@@ -1284,13 +1333,14 @@
         w_gate,
         w_up,
         w_down.T,
-        jnp.concatenate([attn_gain, mlp_gain]).astype(F32)[None],
+        attn_gain[None],
+        mlp_gain[None],
         layer_input,
         out_grad,
         query_gain[None],
         key_gain[None],
         seq_lengths,
-        jnp.concatenate([frequency, frequency])[None],
+        np.concatenate([frequency, frequency]).astype(np.float32)[None],
     )
     results = list(write_results(*parts))
     for k in (2, 6, 7, 9):

time: 137 us -> 133 us (0.971)
  Pallas kernels: 135 us -> 132 us
    pallas_call x1, Pallas kernels: 132 us -> 130 us  [run_layer(): pl.pallas_call(layer_kernel, out_shape=(sds(block, BF), sds(block, BF), s...]
where the time goes in v4:
time: 133 us
  Pallas kernels  132 us (99%)
    pallas_call x1, Pallas kernels, run_layer(): pl.pallas_call(layer_kernel, out_shape=(sds(block, BF), sds(block, BF), s...  130 us

profile of v4, /device:TPU:1, one launch (start us, length us, event | category | flops | bytes accessed | tf_op | source)
XLA Modules:
  0.0 133.0 jit_solution(13388195157446611269)
XLA Ops:
  0.7 130.0 %layer.1 = (bf16[128,1024]{1,0:T(8,128)(2,1)}, bf16[128,1024]{1,0:T(8,128)(2,1)}, f32[64,256]{1,0:T(8,128)}, f32[64,256]{1,0:T(8,128)}, f32[64,256]{1,0:T(8,128)...) custom-call(bf16[64,256]{1,0:T(8,128)(2,1)} %w_query.1, bf16[64,128]{1,0:T(8,128)(2,1)} %w_key.1, ...), custom_call_target="tpu_custom_call" | custom-call | tf_op jit(solution)/shard_map/layer/pallas_call | solution.py:1223
  130.7 2.2 %results.1 = (bf16[128,1024]{1,0:T(8,128)(2,1)}, bf16[128,1024]{1,0:T(8,128)(2,1)}, f32[1,64]{1,0:T(1,128)}, f32[64,256]{1,0:T(8,128)}, f32[64,128]{1,0:T(8,128)...) custom-call(bf16[128,1024]{1,0:T(8,128)(2,1)} %get-tuple-element.34., ...), custom_call_target="tpu_custom_call" | custom-call | tf_op jit(solution)/shard_map/results/pallas_call | solution.py:1302

commit v5 on v4

--- a/solution.py
+++ b/solution.py
@@ -786,19 +786,7 @@
     gather_o.spread()
     gather_u.begin()
 
-    gather_x.sides()
-    gather_q.third()
-    gather_d.spread()
-    for k in range(1, 4):
-        other = (x + k) % 4
-        links.wait(gain_in.at[pl.ds(other * 4, 4)], place.at(dx=k), gain_x_id + other)
     low = lax.broadcasted_iota(jnp.int32, (1, 128), 1) < 64
-    for k in range(8):
-        even, odd = gain_in[2 * k][0:1], gain_in[2 * k + 1][0:1]
-        cols = slice(128 * k, 128 * k + 128)
-        gain_one[0:1, cols] = jnp.where(low, even, pltpu.roll(odd, 64, 1))
-        gain_two[0:1, cols] = jnp.where(low, pltpu.roll(even, 64, 1), odd)
-
     links.wait(lengths, place.core, lengths_id, when=away)
 
     def trig_chunk(i, carry):
@@ -816,6 +804,19 @@
         return carry
 
     lax.fori_loop(0, 4, trig_chunk, 0)
+
+    gather_x.sides()
+    gather_q.third()
+    gather_d.spread()
+    for k in range(1, 4):
+        other = (x + k) % 4
+        links.wait(gain_in.at[pl.ds(other * 4, 4)], place.at(dx=k), gain_x_id + other)
+    for k in range(8):
+        even, odd = gain_in[2 * k][0:1], gain_in[2 * k + 1][0:1]
+        cols = slice(128 * k, 128 * k + 128)
+        gain_one[0:1, cols] = jnp.where(low, even, pltpu.roll(odd, 64, 1))
+        gain_two[0:1, cols] = jnp.where(low, pltpu.roll(even, 64, 1), odd)
+
 
     def norm_pair(k):
         for core in range(2):
@@ -1046,12 +1047,11 @@
         if qb == 2:
             sum_o.relay()
             weight_u.spread()
-            weight_o.cross()
         if qb == 1:
             for k in (2, 1, 3):
                 sum_3.cross(k, when=c == 1)
             weight_d.spread()
-            weight_o.relay()
+            weight_o.cross()
             links.drain(before_gb)
 
     for k in (2, 1, 3):
@@ -1075,6 +1075,7 @@
     weight_k.begin()
     weight_q.begin()
     sum_3.relay()
+    weight_o.relay()
 
     gg_y[y * 2 + c] = gg[...]
     for dy, dc in column:

time: 133 us -> 131 us (0.985)
    pallas_call x1, Pallas kernels: 130 us -> 128 us  [run_layer(): pl.pallas_call(layer_kernel, out_shape=(sds(block, BF), sds(block, BF), s...]
where the time goes in v5:
time: 131 us
  Pallas kernels  131 us (100%)
    pallas_call x1, Pallas kernels, run_layer(): pl.pallas_call(layer_kernel, out_shape=(sds(block, BF), sds(block, BF), s...  128 us

profile of v5, /device:TPU:1, one launch (start us, length us, event | category | flops | bytes accessed | tf_op | source)
XLA Modules:
  0.0 131.3 jit_solution(3152011360650838302)
XLA Ops:
  0.7 128.3 %layer.1 = (bf16[128,1024]{1,0:T(8,128)(2,1)}, bf16[128,1024]{1,0:T(8,128)(2,1)}, f32[64,256]{1,0:T(8,128)}, f32[64,256]{1,0:T(8,128)}, f32[64,256]{1,0:T(8,128)...) custom-call(bf16[64,256]{1,0:T(8,128)(2,1)} %w_query.1, bf16[64,128]{1,0:T(8,128)(2,1)} %w_key.1, ...), custom_call_target="tpu_custom_call" | custom-call | tf_op jit(solution)/shard_map/layer/pallas_call | solution.py:1224
  129.0 2.2 %results.1 = (bf16[128,1024]{1,0:T(8,128)(2,1)}, bf16[128,1024]{1,0:T(8,128)(2,1)}, f32[1,64]{1,0:T(1,128)}, f32[64,256]{1,0:T(8,128)}, f32[64,128]{1,0:T(8,128)...) custom-call(bf16[128,1024]{1,0:T(8,128)(2,1)} %get-tuple-element.34., ...), custom_call_target="tpu_custom_call" | custom-call | tf_op jit(solution)/shard_map/results/pallas_call | solution.py:1303
